TPU v7x, 128 devices: a whole 4x4x4 slice. The times are simulated.
128 devices in a mesh: shard: 128 (over x, y, z, core).
Axes of the slice: x: 4, y: 4, z: 4, core: 2. Of those that a mesh axis runs over, the one named last changes fastest.
Arguments:
- features: bfloat16 [131072, 128], P('shard'), may hold values from -6 to 6
- conv_weight: bfloat16 [27, 128, 128], replicated, may hold values from -0.125 to 0.125
- down_weight: bfloat16 [8, 128, 256], replicated, may hold values from -0.25 to 0.25
- neighbour_map: int32 [27, 131072], P(None, 'shard'), may hold values from 0 to 1280, as said below
- halo_rows: int32 [4, 8192], P(None, 'shard'), may hold values from 0 to 1024, as said below
- child_map: int32 [8, 32768], P(None, 'shard'), may hold values from 0 to 1152, as said below
- child_rows: int32 [4, 4096], P(None, 'shard'), may hold values from 0 to 1024, as said below
- out_grad: bfloat16 [32768, 256], P('shard'), may hold values from -6 to 6
Outputs:
- coarse: bfloat16 [32768, 256], P('shard')
- input_grad: float32 [131072, 128], P('shard')
- conv_grad: float32 [27, 128, 128], replicated
- down_grad: float32 [8, 128, 256], replicated
Inputs may be any that keep to these rules, and one draw needn't show every extreme that they name: `neighbour_map`: indices into the device's extended fine table: below 1024 a local voxel, 1024 + s*64 + c row c received in slot s, the largest value a missing neighbour. Offset 13 maps every voxel to itself. Rows received in slot s that a map reads are live entries of the sender's list. `halo_rows`: live entries come first in a slot, the rest are 1024; every slot toward a missing device is empty; the slot of offset +1 is full on every device that has a next device. `child_map`: as neighbour_map, for the extended hidden table with 32 rows per slot. `child_rows`: as halo_rows, with 32 rows per slot.
All inputs are finite; a program needn't handle non-finite values.
Results may differ from a plain program's by a relative error of at most 0.006.
Values may be sent and summed in bfloat16 or wider, within the bound.
A program may use at most 64 MiB of HBM per device.

v0:
```python
import math

import jax
import jax.numpy as jnp
from jax import lax
from jax.sharding import PartitionSpec as P


def from_behind(value, axis, by):
    count = lax.axis_size(axis)
    pairs = [(i, i + by) for i in range(count) if 0 <= i + by < count]
    return lax.ppermute(value, axis, pairs)


def offsets_list(slot_count):
    half_count = slot_count // 2
    return [number - half_count for number in range(half_count)] + [
        number + 1 for number in range(half_count)
    ]


def chooser_matrix(index_row, table_rows):
    columns = lax.broadcasted_iota(jnp.int32, (index_row.shape[0], table_rows), 1)
    return (index_row[:, None] == columns).astype(jnp.bfloat16)


def select_rows(extended, neighbours):
    table_rows = extended.shape[0]

    def pick(counter, index_row):
        chooser = chooser_matrix(index_row, table_rows)
        picked = jnp.dot(chooser, extended, preferred_element_type=jnp.float32).astype(
            extended.dtype
        )
        return (counter, picked)

    counter, stacked = lax.scan(pick, jnp.zeros((), jnp.int32), neighbours)
    return stacked


def conv_forward(stacked, weights):

    def accumulate(running, inputs):
        picked, kernel = inputs
        return (running + jnp.dot(picked, kernel, preferred_element_type=jnp.float32), None)

    start_sum = jnp.zeros((stacked.shape[1], weights.shape[2]), jnp.float32)
    result, unused = lax.scan(accumulate, start_sum, (stacked, weights))
    return result


def conv_backward(stacked, neighbours, weights, upstream, table_rows):

    def accumulate(carried, inputs):
        index_row, picked, kernel = inputs
        chooser = chooser_matrix(index_row, table_rows)
        weight_grad = lax.dot_general(
            picked, upstream, (((0,), (0,)), ((), ())), preferred_element_type=jnp.float32
        )
        spread = lax.dot_general(
            chooser, upstream, (((0,), (0,)), ((), ())), preferred_element_type=jnp.float32
        )
        spread_high = spread.astype(jnp.bfloat16)
        spread_low = (spread - spread_high.astype(jnp.float32)).astype(jnp.bfloat16)
        back_high = lax.dot_general(
            spread_high, kernel, (((1,), (1,)), ((), ())), preferred_element_type=jnp.float32
        )
        back_low = lax.dot_general(
            spread_low, kernel, (((1,), (1,)), ((), ())), preferred_element_type=jnp.float32
        )
        return (carried + back_high + back_low, weight_grad)

    start_sum = jnp.zeros((table_rows, weights.shape[1]), jnp.float32)
    return lax.scan(accumulate, start_sum, (neighbours, stacked, weights))


def silu_slope(values):
    sigmoid_value = jax.nn.sigmoid(values)
    return sigmoid_value * (1.0 + values * (1.0 - sigmoid_value))


def deliver(blocks, offsets, mover):
    return jnp.stack([mover(blocks[number], offsets[number]) for number in range(len(offsets))])


def add_returned(returned, row_lists, voxels):
    gathered_sum = jnp.zeros((voxels + 1, returned.shape[-1]), jnp.float32)
    for number in range(returned.shape[0]):
        gathered_sum = gathered_sum.at[row_lists[number]].add(returned[number])
    return gathered_sum[:voxels]


def local(
    features, conv_weight, down_weight, neighbour_map, halo_rows, child_map, child_rows, out_grad
):
    voxels = features.shape[0]
    channels = features.shape[1]
    slot_count = halo_rows.shape[0]
    face_cap = halo_rows.shape[1]
    child_cap = child_rows.shape[1]
    offsets = offsets_list(slot_count)
    backward_offsets = [-value for value in offsets]
    devices = lax.axis_size("shard")
    zero_row = jnp.zeros((1, channels), features.dtype)

    def move_face(block, by):
        return from_behind(block, "shard", by)

    def move_child(block, by):
        return from_behind(block, "shard", by)

    def move_child_grad(block, by):
        return from_behind(block, "shard", by)

    def move_face_grad(block, by):
        return from_behind(block.astype(jnp.bfloat16), "shard", by).astype(block.dtype)

    outgoing = jnp.take(jnp.concatenate([features, zero_row]), halo_rows, axis=0)
    incoming = deliver(outgoing, offsets, move_face)
    ext_x = jnp.concatenate([features, incoming.reshape(slot_count * face_cap, channels), zero_row])
    stacked_x = select_rows(ext_x, neighbour_map)
    pre_act = conv_forward(stacked_x, conv_weight)
    hidden = (features.astype(jnp.float32) + jax.nn.silu(pre_act)).astype(jnp.bfloat16)
    leaving = jnp.take(jnp.concatenate([hidden, zero_row]), child_rows, axis=0)
    incoming_h = deliver(leaving, offsets, move_child)
    ext_h = jnp.concatenate(
        [hidden, incoming_h.reshape(slot_count * child_cap, channels), zero_row]
    )
    stacked_h = select_rows(ext_h, child_map)
    lowered = conv_forward(stacked_h, down_weight).astype(jnp.bfloat16)
    back_h, down_terms = conv_backward(stacked_h, child_map, down_weight, out_grad, ext_h.shape[0])
    back_h_slots = back_h[voxels : voxels + slot_count * child_cap].reshape(
        slot_count, child_cap, channels
    )
    returned_h = deliver(back_h_slots, backward_offsets, move_child_grad)
    hidden_grad = back_h[:voxels] + add_returned(returned_h, child_rows, voxels)
    pre_grad = (hidden_grad * silu_slope(pre_act)).astype(jnp.bfloat16)
    back_x, conv_terms = conv_backward(
        stacked_x, neighbour_map, conv_weight, pre_grad, ext_x.shape[0]
    )
    back_x_slots = back_x[voxels : voxels + slot_count * face_cap].reshape(
        slot_count, face_cap, channels
    )
    returned_x = deliver(back_x_slots, backward_offsets, move_face_grad)
    input_grad = hidden_grad + back_x[:voxels] + add_returned(returned_x, halo_rows, voxels)
    conv_summed, down_summed = lax.psum((conv_terms, down_terms), "shard")
    grad_scale = 1.0 / math.sqrt(voxels * devices)
    return (lowered, input_grad, conv_summed * grad_scale, down_summed * grad_scale)


def solution(mesh):
    return jax.shard_map(
        local,
        mesh=mesh,
        in_specs=(
            P("shard", None),
            P(),
            P(),
            P(None, "shard"),
            P(None, "shard"),
            P(None, "shard"),
            P(None, "shard"),
            P("shard", None),
        ),
        out_specs=(P("shard", None), P("shard", None), P(), P()),
        check_vma=False,
    )
```

profile of v0, /device:TPU:1, one launch (start us, length us, event | category | flops | bytes accessed | tf_op | source)
XLA Modules:
  0.0 588.1 jit_solution(8854989896216657970)
XLA Ops:
  10.6 4.9 collective-permute-start.2
  15.6 3.5 collective-permute-start.3
  20.4 1.9 collective-permute-start.1
  26.5 70.7 %while.68 = (s32[]{:T(128)}, bf16[27,1024,128]{2,1,0:T(8,128)(2,1)}, s32[27,1024]{1,0:T(8,128)}, bf16[1281,128]{1,0:T(8,128)(2,1)S(1)}, s32[]{:T(128)}) while((s32[]{:T(128)}, bf16[27,1024,128]{2,1,0:T(8,128)(2,1)}, s32[27,1024]{1,0:T(8,128)}, bf16[1281,128]{1,0:T(8,128)(2,1)S(1)}, s32[]{:T(128)}) %tuple.121), condition=%wide.region_1.2_spmd, body=%wide.region_0.1_spmd.sunk | while | flops 337249280 | bytes 602945 | solution.py:37
  45.6 1.9 fusion.100
  53.4 1.9 fusion.100
  56.0 1.9 fusion.100
  58.7 1.9 fusion.100
  61.3 1.9 fusion.100
  63.9 1.9 fusion.100
  71.8 1.9 fusion.100
  82.3 1.9 fusion.100
  84.9 1.9 fusion.100
  97.2 33.8 %while.70 = (s32[]{:T(128)}, f32[1024,128]{1,0:T(8,128)S(1)}, bf16[27,1024,128]{2,1,0:T(8,128)(2,1)}, bf16[27,128,128]{2,1,0:T(8,128)(2,1)}, s32[]{:T(128)}, /*index=5*/s32[]{:T(128)}) while((s32[]{:T(128)}, f32[1024,128]{1,0:T(8,128)S(1)}, bf16[27,1024,128]{2,1,0:T(8,128)(2,1)}, bf16[27,128,128]{2,1,0:T(8,128)(2,1)}, s32[]{:T(128)}, ...), condition=%wide.region_3.4_spmd.clone, body=%wide.region_2.3_spmd.clone.sunk | while | flops 33816576 | bytes 1344591 | solution.py:48
  133.3 1.9 collective-permute-start.5
  135.2 3.6 collective-permute-start.6
  138.9 4.6 collective-permute-start.7
  144.3 13.9 %while.69 = (s32[]{:T(128)}, bf16[8,256,128]{2,1,0:T(8,128)(2,1)}, s32[8,256]{1,0:T(8,128)}, bf16[1153,128]{1,0:T(8,128)(2,1)S(1)}, s32[]{:T(128)}) while((s32[]{:T(128)}, bf16[8,256,128]{2,1,0:T(8,128)(2,1)}, s32[8,256]{1,0:T(8,128)}, bf16[1153,128]{1,0:T(8,128)(2,1)S(1)}, s32[]{:T(128)}) %tuple.127), condition=%wide.region_5.6_spmd, body=%wide.region_4.5_spmd.sunk | while | flops 75890944 | bytes 364353 | solution.py:37
  158.2 42.6 %while.72 = (s32[]{:T(128)}, f32[1153,128]{1,0:T(8,128)S(1)}, f32[8,128,256]{2,1,0:T(8,128)}, s32[8,256]{1,0:T(8,128)}, bf16[256,256]{1,0:T(8,128)(2,1)S(1)}, /*...) while((s32[]{:T(128)}, f32[1153,128]{1,0:T(8,128)S(1)}, ...), condition=%wide.region_9.10_spmd.clone, body=%wide.region_8.9_spmd.clone.sunk | while | flops 321243008 | bytes 6498411 | solution.py:74
  200.8 3.6 collective-permute-start.8
  204.4 3.6 collective-permute-start.9
  208.0 1.9 collective-permute-start.10
  217.7 179.3 %while.73 = (s32[]{:T(128)}, f32[1281,128]{1,0:T(8,128)S(1)}, f32[27,128,128]{2,1,0:T(8,128)}, s32[27,1024]{1,0:T(8,128)}, bf16[1024,128]{1,0:T(8,128)(2,1)S(1)}...) while((s32[]{:T(128)}, f32[1281,128]{1,0:T(8,128)S(1)}, ...), condition=%wide.region_15.16_spmd.clone, body=%wide.region_14.15_spmd.clone.sunk | while | flops 455936000 | bytes 5523051 | solution.py:74
  222.5 1.9 fusion.122
  229.1 1.9 fusion.122
  235.8 1.9 fusion.122
  397.0 6.1 %collective-permute-start.12 = (bf16[64,128]{1,0:T(8,128)(2,1)S(1)}, bf16[64,128]{1,0:T(8,128)(2,1)S(1)}, u32[]{:S(2)}, u32[]{:S(2)}) collective-permute-start(bf16[64,128]{1,0:T(8,128)(2,1)S(1)} %get-tuple-element.323), channel_id=1, source_target_pairs={{0,2},{1,3},{2,4},{3,5},{4,6},{5,7},{6,8},{7,9},{8,10},{9,11},{10,... | collective-permute-start | bytes 49160 | tf_op jit(solution)/shard_map/ppermute | solution.py:12
  403.2 4.8 collective-permute-start.13
  408.0 1.9 collective-permute-start.14
  411.2 8.8 %while.71 = (s32[]{:T(128)}, f32[256,256]{1,0:T(8,128)S(1)}, bf16[8,256,128]{2,1,0:T(8,128)(2,1)}, bf16[8,128,256]{2,1,0:T(8,128)(2,1)}, s32[]{:T(128)}, /*index=5*/s32[]{:T(128)}) while((s32[]{:T(128)}, f32[256,256]{1,0:T(8,128)S(1)}, bf16[8,256,128]{2,1,0:T(8,128)(2,1)}, bf16[8,128,256]{2,1,0:T(8,128)(2,1)}, s32[]{:T(128)}, ...), condition=%wide.region_7.8_spmd.clone, body=%wide.region_6.7_spmd.clone.sunk | while | flops 16908292 | bytes 656463 | solution.py:48
  426.0 151.2 %all-reduce.5.cloned.1.call-done = (f32[27,128,128]{2,1,0:T(8,128)}, f32[8,128,256]{2,1,0:T(8,128)}) async-done(((f32[27,128,128]{2,1,0:T(8,128)}, f32[8,128,256]{2,1,0:T(8,128)}), (f32[27,128,128]{2,1,0:T(8,128)}, f32[8,128,256]{2,1,0:T(8,128)})) %all-reduce.5.cloned.1.call-update) | async-done | bytes 2818064 | tf_op jit(solution)/shard_map/psum | solution.py:146
  577.2 3.0 broadcast_multiply_fusion
  (347 shorter events, 353.0 us)
Async XLA Ops:
  7.2 570.0 %all-reduce.5.cloned.1.call-start = ((), (), s32[]{:S(2)}) async-start(), calls=%async_computation | async-start | bytes 5636096 | tf_op jit(solution)/shard_map/psum | solution.py:146
  10.6 13.2 %collective-permute-start.2 = (bf16[64,128]{1,0:T(8,128)(2,1)S(1)}, bf16[64,128]{1,0:T(8,128)(2,1)S(1)}, u32[]{:S(2)}, u32[]{:S(2)}) collective-permute-start(bf16[64,128]{1,0:T(8,128)(2,1)S(1)} %get-tuple-element.326), channel_id=1, source_target_pairs={{0,1},{1,2},{2,3},{3,4},{4,5},{5,6},{6,7},{7,8},{8,9},{9,10},{10,1... | collective-permute-start | bytes 49160 | tf_op jit(solution)/shard_map/ppermute | solution.py:12
  15.6 8.3 %collective-permute-start.3 = (bf16[64,128]{1,0:T(8,128)(2,1)S(1)}, bf16[64,128]{1,0:T(8,128)(2,1)S(1)}, u32[]{:S(2)}, u32[]{:S(2)}) collective-permute-start(bf16[64,128]{1,0:T(8,128)(2,1)S(1)} %get-tuple-element.325), channel_id=1, source_target_pairs={{0,2},{1,3},{2,4},{3,5},{4,6},{5,7},{6,8},{7,9},{8,10},{9,11},{10,... | collective-permute-start | bytes 49160 | tf_op jit(solution)/shard_map/ppermute | solution.py:12
  19.1 4.7 collective-permute-start
  20.4 5.1 collective-permute-start.1
  97.2 33.8 %copy-start.1 = (bf16[1024,128]{1,0:T(8,128)(2,1)S(1)}, bf16[1024,128]{1,0:T(8,128)(2,1)}, u32[]{:S(2)}) copy-start(bf16[1024,128]{1,0:T(8,128)(2,1)} %param.20) | copy-start | bytes 786436
  131.0 12.5 %copy-start.3 = (s32[4,32]{1,0:T(4,128)S(1)}, s32[4,32]{1,0:T(4,128)}, u32[]{:S(2)}) copy-start(s32[4,32]{1,0:T(4,128)} %param.26) | copy-start | bytes 1540
  132.0 11.6 %collective-permute-start.4 = (bf16[32,128]{1,0:T(8,128)(2,1)S(1)}, bf16[32,128]{1,0:T(8,128)(2,1)S(1)}, u32[]{:S(2)}, u32[]{:S(2)}) collective-permute-start(bf16[32,128]{1,0:T(8,128)(2,1)S(1)} %get-tuple-element.328), channel_id=1, source_target_pairs={{2,0},{3,1},{4,2},{5,3},{6,4},{7,5},{8,6},{9,7},{10,8},{11,9},{12,... | collective-permute-start | bytes 24584 | tf_op jit(solution)/shard_map/ppermute | solution.py:12
  133.3 10.3 %collective-permute-start.5 = (bf16[32,128]{1,0:T(8,128)(2,1)S(1)}, bf16[32,128]{1,0:T(8,128)(2,1)S(1)}, u32[]{:S(2)}, u32[]{:S(2)}) collective-permute-start(bf16[32,128]{1,0:T(8,128)(2,1)S(1)} %get-tuple-element.331), channel_id=1, source_target_pairs={{1,0},{2,1},{3,2},{4,3},{5,4},{6,5},{7,6},{8,7},{9,8},{10,9},{11,1... | collective-permute-start | bytes 24584 | tf_op jit(solution)/shard_map/ppermute | solution.py:12
  135.2 8.4 %collective-permute-start.6 = (bf16[32,128]{1,0:T(8,128)(2,1)S(1)}, bf16[32,128]{1,0:T(8,128)(2,1)S(1)}, u32[]{:S(2)}, u32[]{:S(2)}) collective-permute-start(bf16[32,128]{1,0:T(8,128)(2,1)S(1)} %get-tuple-element.330), channel_id=1, source_target_pairs={{0,1},{1,2},{2,3},{3,4},{4,5},{5,6},{6,7},{7,8},{8,9},{9,10},{10,1... | collective-permute-start | bytes 24584 | tf_op jit(solution)/shard_map/ppermute | solution.py:12
  138.9 5.4 collective-permute-start.7
  144.3 13.9 %copy-start = (bf16[256,256]{1,0:T(8,128)(2,1)S(1)}, bf16[256,256]{1,0:T(8,128)(2,1)}, u32[]{:S(2)}) copy-start(bf16[256,256]{1,0:T(8,128)(2,1)} %param.27) | copy-start | bytes 393220
  158.2 53.0 %copy-start.4 = (s32[4,64]{1,0:T(4,128)S(1)}, s32[4,64]{1,0:T(4,128)}, u32[]{:S(2)}) copy-start(s32[4,64]{1,0:T(4,128)} %param.24) | copy-start | bytes 3076
  200.8 10.5 %collective-permute-start.8 = (f32[32,128]{1,0:T(8,128)S(1)}, f32[32,128]{1,0:T(8,128)S(1)}, u32[]{:S(2)}, u32[]{:S(2)}) collective-permute-start(f32[32,128]{1,0:T(8,128)S(1)} %get-tuple-element.318), channel_id=1, source_target_pairs={{0,2},{1,3},{2,4},{3,5},{4,6},{5,7},{6,8},{7,9},{8,10},{9,11},{10,... | collective-permute-start | bytes 49160 | tf_op jit(solution)/shard_map/ppermute | solution.py:12
  204.4 7.8 %collective-permute-start.9 = (f32[32,128]{1,0:T(8,128)S(1)}, f32[32,128]{1,0:T(8,128)S(1)}, u32[]{:S(2)}, u32[]{:S(2)}) collective-permute-start(f32[32,128]{1,0:T(8,128)S(1)} %get-tuple-element.317), channel_id=1, source_target_pairs={{0,1},{1,2},{2,3},{3,4},{4,5},{5,6},{6,7},{7,8},{8,9},{9,10},{10,1... | collective-permute-start | bytes 49160 | tf_op jit(solution)/shard_map/ppermute | solution.py:12
  208.0 6.0 %collective-permute-start.10 = (f32[32,128]{1,0:T(8,128)S(1)}, f32[32,128]{1,0:T(8,128)S(1)}, u32[]{:S(2)}, u32[]{:S(2)}) collective-permute-start(f32[32,128]{1,0:T(8,128)S(1)} %get-tuple-element.319), channel_id=1, source_target_pairs={{1,0},{2,1},{3,2},{4,3},{5,4},{6,5},{7,6},{8,7},{9,8},{10,9},{11,1... | collective-permute-start | bytes 49160 | tf_op jit(solution)/shard_map/ppermute | solution.py:12
  209.9 6.6 %collective-permute-start.11 = (f32[32,128]{1,0:T(8,128)S(1)}, f32[32,128]{1,0:T(8,128)S(1)}, u32[]{:S(2)}, u32[]{:S(2)}) collective-permute-start(f32[32,128]{1,0:T(8,128)S(1)} %get-tuple-element.316), channel_id=1, source_target_pairs={{2,0},{3,1},{4,2},{5,3},{6,4},{7,5},{8,6},{9,7},{10,8},{11,9},{12,... | collective-permute-start | bytes 49160 | tf_op jit(solution)/shard_map/ppermute | solution.py:12
  397.0 23.7 %collective-permute-start.12 = (bf16[64,128]{1,0:T(8,128)(2,1)S(1)}, bf16[64,128]{1,0:T(8,128)(2,1)S(1)}, u32[]{:S(2)}, u32[]{:S(2)}) collective-permute-start(bf16[64,128]{1,0:T(8,128)(2,1)S(1)} %get-tuple-element.323), channel_id=1, source_target_pairs={{0,2},{1,3},{2,4},{3,5},{4,6},{5,7},{6,8},{7,9},{8,10},{9,11},{10,... | collective-permute-start | bytes 49160 | tf_op jit(solution)/shard_map/ppermute | solution.py:12
  403.2 18.7 %collective-permute-start.13 = (bf16[64,128]{1,0:T(8,128)(2,1)S(1)}, bf16[64,128]{1,0:T(8,128)(2,1)S(1)}, u32[]{:S(2)}, u32[]{:S(2)}) collective-permute-start(bf16[64,128]{1,0:T(8,128)(2,1)S(1)} %get-tuple-element.322), channel_id=1, source_target_pairs={{0,1},{1,2},{2,3},{3,4},{4,5},{5,6},{6,7},{7,8},{8,9},{9,10},{10,1... | collective-permute-start | bytes 49160 | tf_op jit(solution)/shard_map/ppermute | solution.py:12
  408.0 15.0 %collective-permute-start.14 = (bf16[64,128]{1,0:T(8,128)(2,1)S(1)}, bf16[64,128]{1,0:T(8,128)(2,1)S(1)}, u32[]{:S(2)}, u32[]{:S(2)}) collective-permute-start(bf16[64,128]{1,0:T(8,128)(2,1)S(1)} %get-tuple-element.321), channel_id=1, source_target_pairs={{1,0},{2,1},{3,2},{4,3},{5,4},{6,5},{7,6},{8,7},{9,8},{10,9},{11,1... | collective-permute-start | bytes 49160 | tf_op jit(solution)/shard_map/ppermute | solution.py:12
  409.9 14.1 %collective-permute-start.15 = (bf16[64,128]{1,0:T(8,128)(2,1)S(1)}, bf16[64,128]{1,0:T(8,128)(2,1)S(1)}, u32[]{:S(2)}, u32[]{:S(2)}) collective-permute-start(bf16[64,128]{1,0:T(8,128)(2,1)S(1)} %get-tuple-element.320), channel_id=1, source_target_pairs={{2,0},{3,1},{4,2},{5,3},{6,4},{7,5},{8,6},{9,7},{10,8},{11,9},{12,... | collective-permute-start | bytes 49160 | tf_op jit(solution)/shard_map/ppermute | solution.py:12
  577.2 3.0 copy-start.2
Sparse Core Ops, SparseCore 0:
  411.3 165.8 all-reduce.4
where the time goes:
time: 600 us; the launch traced here: 588 us
  matrix products  295 us (49%)
  waiting for transfers between devices  156 us (26%)
  local copies, waits for them, and re-layouts  55.3 us (9%)
  starting transfers between devices  47.7 us (8%)
  other arithmetic  18 us (3%)
  between operations  14.5 us (2%)
    psum x1, waiting for transfers between devices, local(): conv_summed, down_summed = lax.psum((conv_terms, down_terms), 'shard')  151 us
    dot_general x35, matrix products, accumulate(): lax.dot_general(picked, upstream, (((0,), (0,)), ((), ())), preferred_ele...  63.7 us
    dot_general x35, matrix products, pick(): jnp.dot(chooser, extended, preferred_element_type=jnp.float32)  58.3 us
    dot_general x35, matrix products, accumulate(): lax.dot_general(chooser, upstream, (((0,), (0,)), ((), ())), preferred_el...  53.4 us
    dynamic_slice x70, local copies, waits for them, and re-layouts, select_rows(): counter, stacked = lax.scan(pick, jnp.zeros((), jnp.int32), neighbours)  52.5 us
    ppermute x16, starting transfers between devices, from_behind(): return lax.ppermute(value, axis, pairs)  47.7 us
    dot_general x35, matrix products, accumulate(): jnp.dot(picked, kernel, preferred_element_type=jnp.float32)  41.8 us
    dot_general x35, matrix products, accumulate(): lax.dot_general(spread_low, kernel, (((1,), (1,)), ((), ())), preferred_e...  39 us
  transfers between devices with their start and end apart: 17, of which 5 were waited for; matrix products, arithmetic and copies ran while one was open for 3% of the time, Pallas kernels for 0%

commit v1 on v0

v1 whole, which is shorter than its diff:
```python
import math

import jax
import jax.numpy as jnp
from jax import lax
from jax.experimental import pallas as pl
from jax.experimental.pallas import tpu as pltpu
from jax.sharding import PartitionSpec as P

MESH = pl.DeviceIdType.MESH
BF = jnp.bfloat16
F32 = jnp.float32
K = 27
O = 8
V = 1024
PD = 256
C = 128
C2 = 256
S = 4
CAP = 64
CAP2 = 32
HALF = V // 2
PAIRS = HALF + 128
OFFSETS = (-2, -1, 1, 2)


def row_codes(rows, last, fold_received):
    received = rows >= V
    in_received = (rows >> 7) & 1 if fold_received else jnp.zeros_like(rows)
    side = jnp.where(received, in_received, (rows >> 9) & 1)
    block = jnp.where(received, 4, (rows >> 7) & 3)
    code = ((rows & 127) + 128) << block
    code = jnp.where(side == 1, -code, code)
    return jnp.where(rows >= last, 0, code).astype(F32)


def table_codes(shape, dim, start=0):
    place = lax.broadcasted_iota(jnp.int32, shape, dim) + start
    return (((place & 127) + 128) << (place >> 7)).astype(F32).astype(BF)


def pick_matrix(codes):
    size = jnp.abs(codes)
    names = table_codes((1, PAIRS), 1)
    one, zero = jnp.ones((), BF), jnp.zeros((), BF)
    return jnp.concatenate(
        [jnp.where(size == names[:, b * 128 : (b + 1) * 128], one, zero) for b in range(PAIRS // 128)], axis=1
    )


def spread_matrix(row, start, count):
    n = row.shape[1]
    size = jnp.broadcast_to(jnp.abs(row), (count, n)).astype(BF)
    names = table_codes((count, 128), 0, start)
    names = jnp.concatenate([names] * (n // 128), axis=1)
    return jnp.where(size == names, jnp.ones((), BF), jnp.zeros((), BF))


def pick_side(both, codes):
    both = both.astype(BF)
    return jnp.where(codes < 0, both[:, C:], both[:, :C])


def two_sides(rows, codes):
    zero = jnp.zeros((), BF)
    return jnp.concatenate([jnp.where(codes >= 0, rows, zero), jnp.where(codes < 0, rows, zero)], axis=1)


def dot(a, b):
    return jnp.dot(a, b, preferred_element_type=F32)


def dot_t(a, b):
    return lax.dot_general(a, b, (((1,), (1,)), ((), ())), preferred_element_type=F32)


def t_dot(a, b):
    return lax.dot_general(a, b, (((0,), (0,)), ((), ())), preferred_element_type=F32)


def list_matrix(lists, cap):
    row = jnp.concatenate([lists[s : s + 1, :] for s in range(S)], axis=1)
    places = lax.broadcasted_iota(jnp.int32, (V, S * cap), 0)
    return (places == row).astype(F32).astype(BF)


def kernel(
    features, conv_weight, down_weight, neighbour_map, halo_rows, child_map, child_rows, out_grad,
    coarse, input_grad, conv_terms, down_terms,
    codes_x, wide_x, codes_h, wide_h, picked, table, pre, hidden, hidden_grad, pre_grad, z_all, back_x, back_h,
    out_x, in_x, out_h, in_h, out_gh, in_gh, out_gx, in_gx, send_sem, recv_sem,
):
    n = lax.axis_size("shard")
    me = lax.axis_index("shard")

    def device(by):
        return (lax.rem(me + by + n, n),)

    barrier = pltpu.get_barrier_semaphore()
    for by in OFFSETS:
        pl.semaphore_signal(barrier, inc=1, device_id=device(by), device_id_type=MESH)

    def copies(which, src, dst, sign):
        return [
            pltpu.make_async_remote_copy(
                src_ref=src.at[s],
                dst_ref=dst.at[s],
                send_sem=send_sem.at[which, s],
                recv_sem=recv_sem.at[which, s],
                device_id=device(sign * OFFSETS[s]),
                device_id_type=MESH,
            )
            for s in range(S)
        ]

    chosen = t_dot(list_matrix(halo_rows[...], CAP), features[...]).astype(BF)
    for s in range(S):
        out_x[s] = chosen[s * CAP : (s + 1) * CAP]
    pl.semaphore_wait(barrier, S)
    send_x = copies(0, out_x, in_x, 1)
    for copy in send_x:
        copy.start()

    codes_h[...] = row_codes(child_map[...], V + S * CAP2, False)
    codes_turned = [codes_h[:, b * 128 : (b + 1) * 128].T for b in range(PD // 128)]
    for o in range(O):
        for b in range(PD // 128):
            wide_h[pl.ds(o * PD + b * 128, 128), :] = jnp.broadcast_to(codes_turned[b][:, o : o + 1], (128, 128)).astype(BF)
    for o in range(O):
        z = dot_t(out_grad[...], down_weight[o]).astype(BF)
        z_all[o, 0:PD, :] = two_sides(z, wide_h[pl.ds(o * PD, PD), :])
    total = jnp.zeros((PAIRS, 2 * C), F32)
    for o in range(O):
        total += dot(spread_matrix(codes_h[o : o + 1, :], 0, PAIRS), z_all[o, 0:PD, :])
    back_h[...] = total
    for s in range(S):
        out_gh[s] = back_h[pl.ds(HALF + s * CAP2, CAP2), 0:C].astype(BF)
    send_gh = copies(1, out_gh, in_gh, -1)
    for copy in send_gh:
        copy.start()

    codes_x[0:K, :] = row_codes(neighbour_map[...], V + S * CAP, True)
    codes_x[K:32, :] = jnp.zeros((32 - K, V), F32)

    def widen(b, carry):
        at = pl.ds(pl.multiple_of(b * 128, 128), 128)
        turned = codes_x[:, at].T
        for k in range(K):
            wide_x[k, at, :] = jnp.broadcast_to(turned[:, k : k + 1], (128, 128)).astype(BF)
        return carry

    lax.fori_loop(0, V // 128, widen, 0)

    table[0:HALF, 0:C] = features[0:HALF, :]
    table[0:HALF, C : 2 * C] = features[HALF:V, :]
    for copy in send_x:
        copy.wait_recv()
    for s in range(S):
        table[pl.ds(HALF + (s % 2) * CAP, CAP), pl.ds((s // 2) * C, C)] = in_x[s]
    pre[...] = jnp.zeros_like(pre)

    def forward(k, carry):
        codes = wide_x[k]
        rows = pick_side(dot(pick_matrix(codes), table[...]), codes)
        picked[k] = rows
        pre[...] += dot(rows, conv_weight[k])
        return carry

    lax.fori_loop(0, K, forward, 0)

    act = pre[...]
    gate = jax.nn.sigmoid(act)
    hidden[...] = (features[...].astype(F32) + act * gate).astype(BF)
    child_pick = list_matrix(child_rows[...], CAP2)
    chosen = t_dot(child_pick, hidden[...]).astype(BF)
    for s in range(S):
        out_h[s] = chosen[s * CAP2 : (s + 1) * CAP2]
    send_h = copies(2, out_h, in_h, 1)
    for copy in send_h:
        copy.start()
    for copy in send_gh:
        copy.wait_recv()
    returned = dot(child_pick, jnp.concatenate([in_gh[s] for s in range(S)], axis=0))
    grad_h = jnp.concatenate([back_h[0:HALF, 0:C], back_h[0:HALF, C : 2 * C]], axis=0) + returned
    hidden_grad[...] = grad_h
    pre_grad[...] = (grad_h * (gate * (1.0 + act * (1.0 - gate)))).astype(BF)

    turned_grad = pre_grad[...].T
    for k in range(0, K, 2):
        count = min(2, K - k)
        terms = dot(turned_grad, jnp.concatenate([picked[k + i] for i in range(count)], axis=1))
        for i in range(count):
            conv_terms[k + i] = terms[:, i * C : (i + 1) * C].T

    back_x[...] = jnp.zeros_like(back_x)

    def backward(k, carry):
        z = dot_t(pre_grad[...], conv_weight[k]).astype(BF)
        z_all[k] = two_sides(z, wide_x[k])
        row = codes_x[pl.ds(k, 1), :]
        back_x[HALF:PAIRS, :] += dot(spread_matrix(row, HALF, 128), z_all[k])
        return carry

    lax.fori_loop(0, K, backward, 0)
    for s in range(S):
        out_gx[s] = back_x[pl.ds(HALF + (s % 2) * CAP, CAP), pl.ds((s // 2) * C, C)].astype(BF)
    send_gx = copies(3, out_gx, in_gx, -1)
    for copy in send_gx:
        copy.start()

    def backward_local(k, carry):
        row = codes_x[pl.ds(k, 1), :]
        back_x[0:HALF, :] += dot(spread_matrix(row, 0, HALF), z_all[k])
        return carry

    lax.fori_loop(0, K, backward_local, 0)

    table[0:HALF, 0:C] = hidden[0:HALF, :]
    table[0:HALF, C : 2 * C] = hidden[HALF:V, :]
    table[HALF:PAIRS, C : 2 * C] = jnp.zeros((128, C), BF)
    for copy in send_h:
        copy.wait_recv()
    for s in range(S):
        table[pl.ds(HALF + s * CAP2, CAP2), 0:C] = in_h[s]
    total = jnp.zeros((PD, C2), F32)
    for o in range(O):
        codes = wide_h[pl.ds(o * PD, PD), :]
        rows = pick_side(dot(pick_matrix(codes), table[...]), codes)
        total += dot(rows, down_weight[o])
        down_terms[o] = t_dot(rows, out_grad[...])
    coarse[...] = total.astype(BF)

    for copy in send_gx:
        copy.wait_recv()
    returned = dot(list_matrix(halo_rows[...], CAP), jnp.concatenate([in_gx[s] for s in range(S)], axis=0))
    local_back = jnp.concatenate([back_x[0:HALF, 0:C], back_x[0:HALF, C : 2 * C]], axis=0)
    input_grad[...] = hidden_grad[...] + local_back + returned

    for copy in send_x + send_gh + send_h + send_gx:
        copy.wait_send()


def local(features, conv_weight, down_weight, neighbour_map, halo_rows, child_map, child_rows, out_grad):
    devices = lax.axis_size("shard")
    coarse, input_grad, conv_terms, down_terms = pl.pallas_call(
        kernel,
        out_shape=(
            jax.ShapeDtypeStruct((PD, C2), BF),
            jax.ShapeDtypeStruct((V, C), F32),
            jax.ShapeDtypeStruct((K, C, C), F32),
            jax.ShapeDtypeStruct((O, C, C2), F32),
        ),
        scratch_shapes=[
            pltpu.VMEM((32, V), F32),
            pltpu.VMEM((K, V, 128), BF),
            pltpu.VMEM((O, PD), F32),
            pltpu.VMEM((O * PD, 128), BF),
            pltpu.VMEM((K, V, C), BF),
            pltpu.VMEM((PAIRS, 2 * C), BF),
            pltpu.VMEM((V, C), F32),
            pltpu.VMEM((V, C), BF),
            pltpu.VMEM((V, C), F32),
            pltpu.VMEM((V, C), BF),
            pltpu.VMEM((K, V, 2 * C), BF),
            pltpu.VMEM((PAIRS, 2 * C), F32),
            pltpu.VMEM((PAIRS, 2 * C), F32),
            pltpu.VMEM((S, CAP, C), BF),
            pltpu.VMEM((S, CAP, C), BF),
            pltpu.VMEM((S, CAP2, C), BF),
            pltpu.VMEM((S, CAP2, C), BF),
            pltpu.VMEM((S, CAP2, C), BF),
            pltpu.VMEM((S, CAP2, C), BF),
            pltpu.VMEM((S, CAP, C), BF),
            pltpu.VMEM((S, CAP, C), BF),
            pltpu.SemaphoreType.DMA((4, S)),
            pltpu.SemaphoreType.DMA((4, S)),
        ],
        compiler_params=pltpu.CompilerParams(
            collective_id=0, has_side_effects=True, vmem_limit_bytes=56 * 2**20
        ),
    )(features, conv_weight, down_weight, neighbour_map, halo_rows, child_map, child_rows, out_grad)
    conv_summed, down_summed = lax.psum((conv_terms, down_terms), "shard")
    grad_scale = 1.0 / math.sqrt(V * devices)
    return (coarse, input_grad, conv_summed * grad_scale, down_summed * grad_scale)


def solution(mesh):
    return jax.shard_map(
        local,
        mesh=mesh,
        in_specs=(
            P("shard", None),
            P(),
            P(),
            P(None, "shard"),
            P(None, "shard"),
            P(None, "shard"),
            P(None, "shard"),
            P("shard", None),
        ),
        out_specs=(P("shard", None), P("shard", None), P(), P()),
        check_vma=False,
    )
```

time: 600 us -> 239 us (0.40); the launches traced: 588 us -> 238 us
  matrix products: 295 us -> 0 us
  Pallas kernels: 0 us -> 68.6 us
  local copies, waits for them, and re-layouts: 55.3 us -> 1.46 us
  starting transfers between devices: 47.7 us -> 0.04 us
  other arithmetic: 18 us -> 4.07 us
  waiting for transfers between devices: 156 us -> 150 us
    dot_general x210 -> x0, matrix products: 295 us -> none  [the longest x35 63.7 us: accumulate(): lax.dot_general(picked, upstream, (((0,), (0,)), ((), ())), preferred_ele...]
    pallas_call x0 -> x1, Pallas kernels: none -> 68.6 us  [local(): pl.pallas_call(kernel, out_shape=(jax.ShapeDtypeStruct((PD, C2), BF), jax...]
    dynamic_slice x70 -> x0, local copies, waits for them, and re-layouts: 52.5 us -> none  [select_rows(): counter, stacked = lax.scan(pick, jnp.zeros((), jnp.int32), neighbours)]
    ppermute x16 -> x0, starting transfers between devices: 47.7 us -> none  [from_behind(): return lax.ppermute(value, axis, pairs)]
    scatter-add x8 -> x0, other arithmetic: 7.9 us -> none  [add_returned(): gathered_sum = gathered_sum.at[row_lists[number]].add(returned[number])]
  transfers between devices with their start and end apart: 17 -> 1, of which waited for: 5 -> 1; matrix products, arithmetic and copies ran while one was open for 3% -> 0% of each run, Pallas kernels for 0% -> 0%
where the time goes in v1:
time: 239 us; the launch traced here: 238 us
  waiting for transfers between devices  150 us (63%)
  Pallas kernels  68.6 us (29%)
  between operations  14 us (6%)
  other arithmetic  4.07 us (2%)
    psum x1, waiting for transfers between devices, local(): conv_summed, down_summed = lax.psum((conv_terms, down_terms), 'shard')  150 us
    pallas_call x1, Pallas kernels, local(): pl.pallas_call(kernel, out_shape=(jax.ShapeDtypeStruct((PD, C2), BF), jax...  68.6 us
  transfers between devices with their start and end apart: 1, of which 1 were waited for; matrix products, arithmetic and copies ran while one was open for 0% of the time, Pallas kernels for 0%

profile of v1, /device:TPU:1, one launch (start us, length us, event | category | flops | bytes accessed | tf_op | source)
XLA Modules:
  0.0 238.4 jit_solution(14507112444267129414)
XLA Ops:
  7.2 0.0 all-reduce.3.cloned.1.call-start
  7.2 68.6 %shard_map.111 = (bf16[256,256]{1,0:T(8,128)(2,1)}, f32[1024,128]{1,0:T(8,128)}, f32[27,128,128]{2,1,0:T(8,128)}, f32[8,128,256]{2,1,0:T(8,128)}) custom-call(bf16[1024,128]{1,0:T(8,128)(2,1)} %features.1, bf16[27,128,128]{2,1,0:T(8,128)(2,1)} %conv_weight.1, bf16[8,128,256]{2,1,0:T(8,128)(2,1)} %down_weight.1, s32[27,1024]{1,0:T(8,128)} %neighbour_map.1, ...), custom_call_target="tpu_custom_call" | custom-call | tf_op jit(solution)/shard_map/pallas_call | solution.py:245
  75.8 0.0 all-reduce.3.cloned.1.call-update
  75.8 150.2 %all-reduce.3.cloned.1.call-done = (f32[27,128,128]{2,1,0:T(8,128)}, f32[8,128,256]{2,1,0:T(8,128)}) async-done(((f32[27,128,128]{2,1,0:T(8,128)}, f32[8,128,256]{2,1,0:T(8,128)}), (f32[27,128,128]{2,1,0:T(8,128)}, f32[8,128,256]{2,1,0:T(8,128)})) %all-reduce.3.cloned.1.call-update) | async-done | bytes 2818064 | tf_op jit(solution)/shard_map/psum | solution.py:282
  226.0 0.0 copy-start
  226.0 3.0 %broadcast_multiply_fusion = f32[27,128,128]{2,1,0:T(8,128)} fusion(f32[27,128,128]{2,1,0:T(8,128)} %get-tuple-element.12), kind=kLoop, calls=%fused_computation | loop fusion | flops 442368 | bytes 3538944 | tf_op jit(solution)/shard_map/mul | solution.py:284
  229.0 0.0 copy-start.2
  229.0 0.0 copy-start.1
  229.0 0.0 copy-done
  229.0 1.1 broadcast_multiply_fusion.1
  230.1 0.0 copy-done.2
  230.1 0.7 copy.16
  230.7 0.0 copy-done.1
  230.7 0.8 copy.17
Async XLA Ops:
  7.2 218.8 %all-reduce.3.cloned.1.call-start = ((), (), s32[]{:S(2)}) async-start(), calls=%async_computation | async-start | bytes 5636096 | tf_op jit(solution)/shard_map/psum | solution.py:282
  226.0 3.0 %copy-start = (f32[8,128,256]{2,1,0:T(8,128)S(1)}, f32[8,128,256]{2,1,0:T(8,128)}, u32[]{:S(2)}) copy-start(f32[8,128,256]{2,1,0:T(8,128)} %get-tuple-element.13) | copy-start | bytes 3145732
  229.0 1.1 copy-start.2
  229.0 1.7 copy-start.1
Sparse Core Ops, SparseCore 0:
  75.9 149.9 all-reduce.2

commit v2 on v1

--- a/solution.py
+++ b/solution.py
@@ -22,6 +22,7 @@
 HALF = V // 2
 PAIRS = HALF + 128
 OFFSETS = (-2, -1, 1, 2)
+AXES = ((2, 8, 32), (8, 32, 2), (32, 2, 8))
 
 
 def row_codes(rows, last, fold_received):
@@ -86,12 +87,18 @@
 
 def kernel(
     features, conv_weight, down_weight, neighbour_map, halo_rows, child_map, child_rows, out_grad,
-    coarse, input_grad, conv_terms, down_terms,
+    coarse, input_grad, summed,
     codes_x, wide_x, codes_h, wide_h, picked, table, pre, hidden, hidden_grad, pre_grad, z_all, back_x, back_h,
     out_x, in_x, out_h, in_h, out_gh, in_gh, out_gx, in_gx, send_sem, recv_sem,
+    terms, got_core, sum_1, got_1, sum_2, got_2, sum_3, got_3, sum_send, sum_recv,
 ):
     n = lax.axis_size("shard")
     me = lax.axis_index("shard")
+    core = lax.rem(me, 2)
+    place = {stride: lax.rem(me // stride, 4) for stride in (2, 8, 32)}
+
+    def along(stride, by):
+        return me + (lax.rem(place[stride] + by, 4) - place[stride]) * stride
 
     def device(by):
         return (lax.rem(me + by + n, n),)
@@ -99,6 +106,11 @@
     barrier = pltpu.get_barrier_semaphore()
     for by in OFFSETS:
         pl.semaphore_signal(barrier, inc=1, device_id=device(by), device_id_type=MESH)
+    sibling = me + 1 - 2 * core
+    pl.semaphore_signal(barrier, inc=1, device_id=(sibling,), device_id_type=MESH)
+    for stride in (2, 8, 32):
+        for by in (1, 2, 3):
+            pl.semaphore_signal(barrier, inc=1, device_id=(along(stride, by),), device_id_type=MESH)
 
     def copies(which, src, dst, sign):
         return [
@@ -113,10 +125,101 @@
             for s in range(S)
         ]
 
+    def remote(src, dst, step, part, lane, to):
+        return pltpu.make_async_remote_copy(
+            src_ref=src,
+            dst_ref=dst,
+            send_sem=sum_send.at[step, part, lane],
+            recv_sem=sum_recv.at[step, part, lane],
+            device_id=(to,),
+            device_id_type=MESH,
+        )
+
+    held = ((sum_1, got_1, 256), (sum_2, got_2, 64), (sum_3, got_3, 16))
+    flying = []
+
+    def spread_step(level, part):
+        stride = AXES[part][level]
+        source, landing, _ = held[level]
+        return [
+            remote(
+                source.at[part, lax.rem(place[stride] + by, 4)], landing.at[part, by - 1], 1 + level, part, by - 1, along(stride, by)
+            )
+            for by in (1, 2, 3)
+        ]
+
+    def start_all(moves):
+        for move in moves:
+            move.start()
+        flying.extend(moves)
+        return moves
+
+    def reduce_start(part):
+        return start_all([remote(terms.at[part, 1 - core], got_core.at[part], 0, part, 0, sibling)])
+
+    def reduce_core(part, moves):
+        for move in moves:
+            move.wait_recv()
+        total = (terms[part, core].astype(F32) + got_core[part].astype(F32)).astype(BF)
+        for q in range(4):
+            sum_1[part, q] = total[q * 256 : (q + 1) * 256]
+        return start_all(spread_step(0, part))
+
+    def reduce_axis(level, part, moves):
+        for move in moves:
+            move.wait_recv()
+        source, landing, _ = held[level]
+        total = source[part, place[AXES[part][level]]].astype(F32)
+        for by in range(3):
+            total += landing[part, by].astype(F32)
+        total = total.astype(BF)
+        if level < 2:
+            target, _, rows = held[level + 1]
+            for q in range(4):
+                target[part, q] = total[q * rows : (q + 1) * rows]
+            return start_all(spread_step(level + 1, part))
+        summed[part, mine(part, 3), :] = total
+        return gather_step(2, part)
+
+    def mine(part, depth):
+        start, size = core * 1024, 1024
+        for level in range(depth):
+            size = size // 4
+            start = start + place[AXES[part][level]] * size
+        return pl.ds(pl.multiple_of(start, 16), size)
+
+    def gather_step(level, part):
+        rows = mine(part, level + 1)
+        return start_all(
+            [
+                remote(summed.at[part, rows], summed.at[part, rows], 6 - level, part, by - 1, along(AXES[part][level], by))
+                for by in (1, 2, 3)
+            ]
+        )
+
+    def gather_axis(level, part, moves):
+        for move in moves:
+            move.wait_recv()
+        if level > 0:
+            return gather_step(level - 1, part)
+        rows = mine(part, 0)
+        return start_all([remote(summed.at[part, rows], summed.at[part, rows], 7, part, 0, sibling)])
+
+    sums = [None] * 3
+
+    def sum_turn(turn):
+        for part in range(3):
+            if turn == 0:
+                sums[part] = reduce_core(part, sums[part])
+            elif turn <= 3:
+                sums[part] = reduce_axis(turn - 1, part, sums[part])
+            else:
+                sums[part] = gather_axis(6 - turn, part, sums[part])
+
     chosen = t_dot(list_matrix(halo_rows[...], CAP), features[...]).astype(BF)
     for s in range(S):
         out_x[s] = chosen[s * CAP : (s + 1) * CAP]
-    pl.semaphore_wait(barrier, S)
+    pl.semaphore_wait(barrier, S + 10)
     send_x = copies(0, out_x, in_x, 1)
     for copy in send_x:
         copy.start()
@@ -188,9 +291,33 @@
     turned_grad = pre_grad[...].T
     for k in range(0, K, 2):
         count = min(2, K - k)
-        terms = dot(turned_grad, jnp.concatenate([picked[k + i] for i in range(count)], axis=1))
+        products = dot(turned_grad, jnp.concatenate([picked[k + i] for i in range(count)], axis=1))
         for i in range(count):
-            conv_terms[k + i] = terms[:, i * C : (i + 1) * C].T
+            block = k + i
+            terms[block // 16, (block // 8) % 2, pl.ds(block % 8 * C, C), :] = products[:, i * C : (i + 1) * C].T.astype(BF)
+    for block in range(K, 32):
+        terms[block // 16, (block // 8) % 2, pl.ds(block % 8 * C, C), :] = jnp.zeros((C, C), BF)
+    sums[0] = reduce_start(0)
+    sums[1] = reduce_start(1)
+
+    table[0:HALF, 0:C] = hidden[0:HALF, :]
+    table[0:HALF, C : 2 * C] = hidden[HALF:V, :]
+    table[HALF:PAIRS, C : 2 * C] = jnp.zeros((128, C), BF)
+    for copy in send_h:
+        copy.wait_recv()
+    for s in range(S):
+        table[pl.ds(HALF + s * CAP2, CAP2), 0:C] = in_h[s]
+    total = jnp.zeros((PD, C2), F32)
+    for o in range(O):
+        codes = wide_h[pl.ds(o * PD, PD), :]
+        rows = pick_side(dot(pick_matrix(codes), table[...]), codes)
+        total += dot(rows, down_weight[o])
+        products = t_dot(rows, out_grad[...]).astype(BF)
+        terms[2, o // 4, pl.ds(o % 4 * 2 * C, C), :] = products[:, 0:C]
+        terms[2, o // 4, pl.ds((o % 4 * 2 + 1) * C, C), :] = products[:, C : 2 * C]
+    coarse[...] = total.astype(BF)
+
+    sums[2] = reduce_start(2)
 
     back_x[...] = jnp.zeros_like(back_x)
 
@@ -201,7 +328,10 @@
         back_x[HALF:PAIRS, :] += dot(spread_matrix(row, HALF, 128), z_all[k])
         return carry
 
-    lax.fori_loop(0, K, backward, 0)
+    lax.fori_loop(0, 9, backward, 0)
+    sum_turn(0)
+    lax.fori_loop(9, K, backward, 0)
+    sum_turn(1)
     for s in range(S):
         out_gx[s] = back_x[pl.ds(HALF + (s % 2) * CAP, CAP), pl.ds((s // 2) * C, C)].astype(BF)
     send_gx = copies(3, out_gx, in_gx, -1)
@@ -213,22 +343,14 @@
         back_x[0:HALF, :] += dot(spread_matrix(row, 0, HALF), z_all[k])
         return carry
 
-    lax.fori_loop(0, K, backward_local, 0)
-
-    table[0:HALF, 0:C] = hidden[0:HALF, :]
-    table[0:HALF, C : 2 * C] = hidden[HALF:V, :]
-    table[HALF:PAIRS, C : 2 * C] = jnp.zeros((128, C), BF)
-    for copy in send_h:
-        copy.wait_recv()
-    for s in range(S):
-        table[pl.ds(HALF + s * CAP2, CAP2), 0:C] = in_h[s]
-    total = jnp.zeros((PD, C2), F32)
-    for o in range(O):
-        codes = wide_h[pl.ds(o * PD, PD), :]
-        rows = pick_side(dot(pick_matrix(codes), table[...]), codes)
-        total += dot(rows, down_weight[o])
-        down_terms[o] = t_dot(rows, out_grad[...])
-    coarse[...] = total.astype(BF)
+    lax.fori_loop(0, 6, backward_local, 0)
+    sum_turn(2)
+    lax.fori_loop(6, 12, backward_local, 0)
+    sum_turn(3)
+    lax.fori_loop(12, 18, backward_local, 0)
+    sum_turn(4)
+    lax.fori_loop(18, K, backward_local, 0)
+    sum_turn(5)
 
     for copy in send_gx:
         copy.wait_recv()
@@ -236,19 +358,22 @@
     local_back = jnp.concatenate([back_x[0:HALF, 0:C], back_x[0:HALF, C : 2 * C]], axis=0)
     input_grad[...] = hidden_grad[...] + local_back + returned
 
-    for copy in send_x + send_gh + send_h + send_gx:
+    sum_turn(6)
+    for part in range(3):
+        for move in sums[part]:
+            move.wait_recv()
+    for copy in send_x + send_gh + send_h + send_gx + flying:
         copy.wait_send()
 
 
 def local(features, conv_weight, down_weight, neighbour_map, halo_rows, child_map, child_rows, out_grad):
     devices = lax.axis_size("shard")
-    coarse, input_grad, conv_terms, down_terms = pl.pallas_call(
+    coarse, input_grad, summed = pl.pallas_call(
         kernel,
         out_shape=(
             jax.ShapeDtypeStruct((PD, C2), BF),
             jax.ShapeDtypeStruct((V, C), F32),
-            jax.ShapeDtypeStruct((K, C, C), F32),
-            jax.ShapeDtypeStruct((O, C, C2), F32),
+            jax.ShapeDtypeStruct((3, 2048, C), BF),
         ),
         scratch_shapes=[
             pltpu.VMEM((32, V), F32),
@@ -274,14 +399,26 @@
             pltpu.VMEM((S, CAP, C), BF),
             pltpu.SemaphoreType.DMA((4, S)),
             pltpu.SemaphoreType.DMA((4, S)),
+            pltpu.VMEM((3, 2, 1024, C), BF),
+            pltpu.VMEM((3, 1024, C), BF),
+            pltpu.VMEM((3, 4, 256, C), BF),
+            pltpu.VMEM((3, 3, 256, C), BF),
+            pltpu.VMEM((3, 4, 64, C), BF),
+            pltpu.VMEM((3, 3, 64, C), BF),
+            pltpu.VMEM((3, 4, 16, C), BF),
+            pltpu.VMEM((3, 3, 16, C), BF),
+            pltpu.SemaphoreType.DMA((8, 3, 3)),
+            pltpu.SemaphoreType.DMA((8, 3, 3)),
         ],
         compiler_params=pltpu.CompilerParams(
             collective_id=0, has_side_effects=True, vmem_limit_bytes=56 * 2**20
         ),
     )(features, conv_weight, down_weight, neighbour_map, halo_rows, child_map, child_rows, out_grad)
-    conv_summed, down_summed = lax.psum((conv_terms, down_terms), "shard")
     grad_scale = 1.0 / math.sqrt(V * devices)
-    return (coarse, input_grad, conv_summed * grad_scale, down_summed * grad_scale)
+    blocks = summed.reshape(48, C, C)
+    conv_grad = blocks[:K].astype(F32) * grad_scale
+    down_grad = blocks[32:].reshape(O, 2, C, C).transpose(0, 2, 1, 3).reshape(O, C, C2).astype(F32) * grad_scale
+    return (coarse, input_grad, conv_grad, down_grad)
 
 
 def solution(mesh):

time: 239 us -> 89.4 us (0.37)
  waiting for transfers between devices: 150 us -> 0 us
  Pallas kernels: 68.6 us -> 83.4 us
  between operations: 14 us -> 0.66 us
    psum x1 -> x0, waiting for transfers between devices: 150 us -> none  [local(): conv_summed, down_summed = lax.psum((conv_terms, down_terms), 'shard')]
    pallas_call x1, Pallas kernels: 68.6 us -> 83.4 us  [local(): pl.pallas_call(kernel, out_shape=(jax.ShapeDtypeStruct((PD, C2), BF), jax...]
  transfers between devices with their start and end apart: 1 -> 0, of which waited for: 1 -> 0; matrix products, arithmetic and copies ran while one was open for 0% -> 0% of each run, Pallas kernels for 0% -> 0%
where the time goes in v2:
time: 89.4 us; the launch traced here: 89.3 us
  Pallas kernels  83.4 us (93%)
  other arithmetic  2.66 us (3%)
  local copies, waits for them, and re-layouts  2.52 us (3%)
    pallas_call x1, Pallas kernels, local(): pl.pallas_call(kernel, out_shape=(jax.ShapeDtypeStruct((PD, C2), BF), jax...  83.4 us

profile of v2, /device:TPU:1, one launch (start us, length us, event | category | flops | bytes accessed | tf_op | source)
XLA Modules:
  0.0 89.3 jit_solution(4016089585498129700)
XLA Ops:
  0.6 83.4 %shard_map.111 = (bf16[256,256]{1,0:T(8,128)(2,1)}, f32[1024,128]{1,0:T(8,128)}, bf16[3,2048,128]{2,1,0:T(8,128)(2,1)}) custom-call(bf16[1024,128]{1,0:T(8,128)(2,1)} %features.1, bf16[27,128,128]{2,1,0:T(8,128)(2,1)} %conv_weight.1, bf16[8,128,256]{2,1,0:T(8,128)(2,1)} %down_weight.1, s32[27,1024]{1,0:T(8,128)} %neighbour_map.1, s32[4,64]{1,0:T(4,128)} %halo_rows.1, ...), custom_call_target="tpu_custom_call" | custom-call | tf_op jit(solution)/shard_map/pallas_call | solution.py:371
  84.1 0.0 copy-start
  84.1 1.2 %convert_multiply_fusion.1 = f32[1,2048,128]{2,1,0:T(8,128)S(1)} fusion(bf16[3,2048,128]{2,1,0:T(8,128)(2,1)} %get-tuple-element.9), kind=kLoop, calls=%fused_computation.2 | loop fusion | flops 524288 | bytes 1572864 | tf_op jit(solution)/shard_map/mul | solution.py:420
  85.3 1.1 %copy.15 = f32[8,2,16,8,128]{4,3,1,2,0:T(8,128)} copy(f32[8,2,16,8,128]{4,3,2,1,0:T(8,128)S(1)} %bitcast.8) | data formatting | bytes 2097152 | tf_op jit(solution)/shard_map/mul | solution.py:420
  86.4 0.0 copy-start.2
  86.4 0.0 copy-start.1
  86.4 0.0 copy-done
  86.4 1.4 %convert_multiply_fusion = f32[27,128,128]{2,1,0:T(8,128)} fusion(bf16[48,128,128]{2,1,0:T(8,128)(2,1)S(1)} %bitcast.9), kind=kLoop, calls=%fused_computation | loop fusion | flops 884736 | bytes 2654208 | tf_op jit(solution)/shard_map/mul | solution.py:419
  87.8 0.0 copy-done.2
  87.8 0.7 copy.18
  88.5 0.0 copy-done.1
  88.5 0.8 copy.19
Async XLA Ops:
  84.1 2.3 %copy-start = (bf16[3,2048,128]{2,1,0:T(8,128)(2,1)S(1)}, bf16[3,2048,128]{2,1,0:T(8,128)(2,1)}, u32[]{:S(2)}) copy-start(bf16[3,2048,128]{2,1,0:T(8,128)(2,1)} %get-tuple-element.9) | copy-start | bytes 4718596
  86.4 1.4 %copy-start.2 = (bf16[256,256]{1,0:T(8,128)(2,1)S(1)}, bf16[256,256]{1,0:T(8,128)(2,1)}, u32[]{:S(2)}) copy-start(bf16[256,256]{1,0:T(8,128)(2,1)} %get-tuple-element.14) | copy-start | bytes 393220
  86.4 2.1 %copy-start.1 = (f32[1024,128]{1,0:T(8,128)S(1)}, f32[1024,128]{1,0:T(8,128)}, u32[]{:S(2)}) copy-start(f32[1024,128]{1,0:T(8,128)} %get-tuple-element.15) | copy-start | bytes 1572868

commit v3 on v1

--- a/solution.py
+++ b/solution.py
@@ -22,6 +22,9 @@
 HALF = V // 2
 PAIRS = HALF + 128
 OFFSETS = (-2, -1, 1, 2)
+PLANES = ((2, 8, 32), (8, 32, 2), (32, 2, 8))
+CHUNK = (64, 48, 64)
+HOPS = [(i, j) for i in (2, 1, 3, 0) for j in (2, 1, 3, 0) if i or j]
 
 
 def row_codes(rows, last, fold_received):
@@ -86,12 +89,19 @@
 
 def kernel(
     features, conv_weight, down_weight, neighbour_map, halo_rows, child_map, child_rows, out_grad,
-    coarse, input_grad, conv_terms, down_terms,
+    coarse, input_grad, summed,
     codes_x, wide_x, codes_h, wide_h, picked, table, pre, hidden, hidden_grad, pre_grad, z_all, back_x, back_h,
     out_x, in_x, out_h, in_h, out_gh, in_gh, out_gx, in_gx, send_sem, recv_sem,
+    terms, got_core, core_sum, got_plane, plane_sum,
+    core_send, core_recv, plane_send, plane_recv, axis_send, axis_recv,
 ):
     n = lax.axis_size("shard")
     me = lax.axis_index("shard")
+    core = lax.rem(me, 2)
+    place = {stride: lax.rem(me // stride, 4) for stride in (2, 8, 32)}
+
+    def shift(stride, by):
+        return (lax.rem(place[stride] + by, 4) - place[stride]) * stride
 
     def device(by):
         return (lax.rem(me + by + n, n),)
@@ -99,6 +109,15 @@
     barrier = pltpu.get_barrier_semaphore()
     for by in OFFSETS:
         pl.semaphore_signal(barrier, inc=1, device_id=device(by), device_id_type=MESH)
+    sibling = me + 1 - 2 * core
+    pl.semaphore_signal(barrier, inc=1, device_id=(sibling,), device_id_type=MESH)
+    for a, b, _ in PLANES:
+        for i, j in HOPS:
+            if i and j:
+                to = me + shift(a, i) + shift(b, j)
+                pl.semaphore_signal(barrier, inc=1, device_id=(to,), device_id_type=MESH)
+        for i in (1, 2, 3):
+            pl.semaphore_signal(barrier, inc=1, device_id=(me + shift(a, i),), device_id_type=MESH)
 
     def copies(which, src, dst, sign):
         return [
@@ -113,13 +132,102 @@
             for s in range(S)
         ]
 
+    flying = []
+
+    def send(src, dst, sems, at, to):
+        move = pltpu.make_async_remote_copy(
+            src_ref=src,
+            dst_ref=dst,
+            send_sem=sems[0].at[at],
+            recv_sem=sems[1].at[at],
+            device_id=(to,),
+            device_id_type=MESH,
+        )
+        return move
+
+    def start_all(moves):
+        for move in moves:
+            move.start()
+        flying.extend(moves)
+        return moves
+
+    core_sems, plane_sems, axis_sems = (core_send, core_recv), (plane_send, plane_recv), (axis_send, axis_recv)
+    sums = [()] * 3
+
+    def put_block(block, value):
+        part = 0 if block < 16 else 1 if block < 28 else 2
+        at = block - (0, 16, 28)[part]
+        per_half = CHUNK[part] // 8
+        terms[part, at // per_half, pl.ds(at % per_half * C, C), :] = value
+
+
+    def sum_turn(turn, parts):
+        for part in parts:
+            for move in sums[part]:
+                move.wait_recv()
+            sums[part] = start_all(sum_step(turn, part))
+
+    def sum_step(turn, part):
+        a, b, c = PLANES[part]
+        size = CHUNK[part]
+        here = place[a] * 4 + place[b]
+        half = pl.ds(0, 16 * size)
+        chunk = pl.ds(0, size)
+        owned = pl.ds(pl.multiple_of(core * (16 * size) + here * size, 16), size)
+        if turn == 0:
+            return [send(terms.at[part, 1 - core, half], got_core.at[part, half], core_sems, (0, part), sibling)]
+        if turn == 1:
+            total = (terms[part, core, half].astype(F32) + got_core[part, half].astype(F32)).astype(BF)
+            for q in range(16):
+                core_sum[part, q, chunk] = total[q * size : (q + 1) * size]
+            return [
+                send(
+                    core_sum.at[part, lax.rem(place[a] + i, 4) * 4 + lax.rem(place[b] + j, 4), chunk],
+                    got_plane.at[part, at, chunk], plane_sems, (0, part, at), me + shift(a, i) + shift(b, j),
+                )
+                for at, (i, j) in enumerate(HOPS)
+            ]
+        if turn == 2:
+            total = core_sum[part, here, chunk].astype(F32)
+            for at in range(15):
+                total += got_plane[part, at, chunk].astype(F32)
+            plane_sum[part, place[c], chunk] = total
+            mine = plane_sum.at[part, place[c], chunk]
+            return [send(mine, mine, axis_sems, (part, i - 1), me + shift(c, i)) for i in (1, 2, 3)]
+        if turn == 3:
+            total = plane_sum[part, 0, chunk] + plane_sum[part, 1, chunk]
+            total += plane_sum[part, 2, chunk] + plane_sum[part, 3, chunk]
+            summed[part, owned] = total.astype(BF)
+            mine = summed.at[part, owned]
+            return [
+                send(mine, mine, plane_sems, (1, part, at), me + shift(a, i) + shift(b, j)) for at, (i, j) in enumerate(HOPS)
+            ]
+        if turn == 4:
+            mine = summed.at[part, pl.ds(pl.multiple_of(core * (16 * size), 16), 16 * size)]
+            return [send(mine, mine, core_sems, (1, part), sibling)]
+        return []
+
     chosen = t_dot(list_matrix(halo_rows[...], CAP), features[...]).astype(BF)
     for s in range(S):
         out_x[s] = chosen[s * CAP : (s + 1) * CAP]
-    pl.semaphore_wait(barrier, S)
+    codes_x[0:K, :] = row_codes(neighbour_map[...], V + S * CAP, True)
+    codes_x[K:32, :] = jnp.zeros((32 - K, V), F32)
+
+    def widen(b, carry):
+        at = pl.ds(pl.multiple_of(b * 128, 128), 128)
+        turned = codes_x[:, at].T
+        for k in range(K):
+            wide_x[k, at, :] = jnp.broadcast_to(turned[:, k : k + 1], (128, 128)).astype(BF)
+        return carry
+
+    lax.fori_loop(0, 6, widen, 0)
+
+    pl.semaphore_wait(barrier, S + 37)
     send_x = copies(0, out_x, in_x, 1)
     for copy in send_x:
         copy.start()
+
+    lax.fori_loop(6, V // 128, widen, 0)
 
     codes_h[...] = row_codes(child_map[...], V + S * CAP2, False)
     codes_turned = [codes_h[:, b * 128 : (b + 1) * 128].T for b in range(PD // 128)]
@@ -139,18 +247,6 @@
     for copy in send_gh:
         copy.start()
 
-    codes_x[0:K, :] = row_codes(neighbour_map[...], V + S * CAP, True)
-    codes_x[K:32, :] = jnp.zeros((32 - K, V), F32)
-
-    def widen(b, carry):
-        at = pl.ds(pl.multiple_of(b * 128, 128), 128)
-        turned = codes_x[:, at].T
-        for k in range(K):
-            wide_x[k, at, :] = jnp.broadcast_to(turned[:, k : k + 1], (128, 128)).astype(BF)
-        return carry
-
-    lax.fori_loop(0, V // 128, widen, 0)
-
     table[0:HALF, 0:C] = features[0:HALF, :]
     table[0:HALF, C : 2 * C] = features[HALF:V, :]
     for copy in send_x:
@@ -159,14 +255,19 @@
         table[pl.ds(HALF + (s % 2) * CAP, CAP), pl.ds((s // 2) * C, C)] = in_x[s]
     pre[...] = jnp.zeros_like(pre)
 
-    def forward(k, carry):
-        codes = wide_x[k]
-        rows = pick_side(dot(pick_matrix(codes), table[...]), codes)
-        picked[k] = rows
-        pre[...] += dot(rows, conv_weight[k])
+    def forward(step, carry):
+        k = step * 3
+        group = []
+        for i in range(3):
+            codes = wide_x[k + i]
+            rows = pick_side(dot(pick_matrix(codes), table[...]), codes)
+            picked[k + i] = rows
+            group.append(rows)
+        weights = conv_weight[pl.ds(k, 3)].reshape(3 * C, C)
+        pre[...] += dot(jnp.concatenate(group, axis=1), weights)
         return carry
 
-    lax.fori_loop(0, K, forward, 0)
+    lax.fori_loop(0, K // 3, forward, 0)
 
     act = pre[...]
     gate = jax.nn.sigmoid(act)
@@ -188,32 +289,27 @@
     turned_grad = pre_grad[...].T
     for k in range(0, K, 2):
         count = min(2, K - k)
-        terms = dot(turned_grad, jnp.concatenate([picked[k + i] for i in range(count)], axis=1))
+        products = dot(turned_grad, jnp.concatenate([picked[k + i] for i in range(count)], axis=1))
         for i in range(count):
-            conv_terms[k + i] = terms[:, i * C : (i + 1) * C].T
+            put_block(k + i, products[:, i * C : (i + 1) * C].T.astype(BF))
+    put_block(K, jnp.zeros((C, C), BF))
+    sum_turn(0, (0, 1))
 
     back_x[...] = jnp.zeros_like(back_x)
 
-    def backward(k, carry):
-        z = dot_t(pre_grad[...], conv_weight[k]).astype(BF)
-        z_all[k] = two_sides(z, wide_x[k])
-        row = codes_x[pl.ds(k, 1), :]
-        back_x[HALF:PAIRS, :] += dot(spread_matrix(row, HALF, 128), z_all[k])
+    def backward(step, carry):
+        k = step * 3
+        z = dot_t(pre_grad[...], conv_weight[pl.ds(k, 3)].reshape(3 * C, C)).astype(BF)
+        total = back_x[HALF:PAIRS, :]
+        for i in range(3):
+            z2 = two_sides(z[:, i * C : (i + 1) * C], wide_x[k + i])
+            z_all[k + i] = z2
+            total += dot(spread_matrix(codes_x[pl.ds(k + i, 1), :], HALF, 128), z2)
+        back_x[HALF:PAIRS, :] = total
         return carry
 
-    lax.fori_loop(0, K, backward, 0)
-    for s in range(S):
-        out_gx[s] = back_x[pl.ds(HALF + (s % 2) * CAP, CAP), pl.ds((s // 2) * C, C)].astype(BF)
-    send_gx = copies(3, out_gx, in_gx, -1)
-    for copy in send_gx:
-        copy.start()
-
-    def backward_local(k, carry):
-        row = codes_x[pl.ds(k, 1), :]
-        back_x[0:HALF, :] += dot(spread_matrix(row, 0, HALF), z_all[k])
-        return carry
-
-    lax.fori_loop(0, K, backward_local, 0)
+    lax.fori_loop(0, 2, backward, 0)
+    sum_turn(1, (0, 1))
 
     table[0:HALF, 0:C] = hidden[0:HALF, :]
     table[0:HALF, C : 2 * C] = hidden[HALF:V, :]
@@ -227,8 +323,39 @@
         codes = wide_h[pl.ds(o * PD, PD), :]
         rows = pick_side(dot(pick_matrix(codes), table[...]), codes)
         total += dot(rows, down_weight[o])
-        down_terms[o] = t_dot(rows, out_grad[...])
+        products = t_dot(rows, out_grad[...]).astype(BF)
+        put_block(28 + 2 * o, products[:, 0:C])
+        put_block(29 + 2 * o, products[:, C : 2 * C])
     coarse[...] = total.astype(BF)
+
+    sum_turn(0, (2,))
+
+    lax.fori_loop(2, 4, backward, 0)
+    sum_turn(1, (2,))
+    lax.fori_loop(4, 7, backward, 0)
+    sum_turn(2, (0, 1))
+    lax.fori_loop(7, K // 3, backward, 0)
+    for s in range(S):
+        out_gx[s] = back_x[pl.ds(HALF + (s % 2) * CAP, CAP), pl.ds((s // 2) * C, C)].astype(BF)
+    send_gx = copies(3, out_gx, in_gx, -1)
+    for copy in send_gx:
+        copy.start()
+
+    def backward_local(step, carry):
+        k = step * 3
+        total = back_x[0:HALF, :]
+        for i in range(3):
+            total += dot(spread_matrix(codes_x[pl.ds(k + i, 1), :], 0, HALF), z_all[k + i])
+        back_x[0:HALF, :] = total
+        return carry
+
+    lax.fori_loop(0, 2, backward_local, 0)
+    sum_turn(3, (0, 1))
+    sum_turn(2, (2,))
+    lax.fori_loop(2, 5, backward_local, 0)
+    sum_turn(3, (2,))
+    lax.fori_loop(5, K // 3, backward_local, 0)
+    sum_turn(4, (0, 1))
 
     for copy in send_gx:
         copy.wait_recv()
@@ -236,19 +363,32 @@
     local_back = jnp.concatenate([back_x[0:HALF, 0:C], back_x[0:HALF, C : 2 * C]], axis=0)
     input_grad[...] = hidden_grad[...] + local_back + returned
 
-    for copy in send_x + send_gh + send_h + send_gx:
+    sum_turn(4, (2,))
+    sum_turn(5, (0, 1, 2))
+    for copy in send_x + send_gh + send_h + send_gx + flying:
         copy.wait_send()
+
+
+def finish(grad_scale, coarse_in, input_grad_in, summed, coarse, input_grad, conv_grad, down_grad):
+    coarse[...] = coarse_in[...]
+    input_grad[...] = input_grad_in[...]
+    for k in range(K):
+        part, at = (0, k) if k < 16 else (1, k - 16)
+        conv_grad[k] = summed[part, at * C : (at + 1) * C, :].astype(F32) * grad_scale
+    for o in range(O):
+        for h in range(2):
+            at = (2 * o + h) * C
+            down_grad[o, :, h * C : (h + 1) * C] = summed[2, at : at + C, :].astype(F32) * grad_scale
 
 
 def local(features, conv_weight, down_weight, neighbour_map, halo_rows, child_map, child_rows, out_grad):
     devices = lax.axis_size("shard")
-    coarse, input_grad, conv_terms, down_terms = pl.pallas_call(
+    coarse, input_grad, summed = pl.pallas_call(
         kernel,
         out_shape=(
             jax.ShapeDtypeStruct((PD, C2), BF),
             jax.ShapeDtypeStruct((V, C), F32),
-            jax.ShapeDtypeStruct((K, C, C), F32),
-            jax.ShapeDtypeStruct((O, C, C2), F32),
+            jax.ShapeDtypeStruct((3, 2048, C), BF),
         ),
         scratch_shapes=[
             pltpu.VMEM((32, V), F32),
@@ -274,14 +414,33 @@
             pltpu.VMEM((S, CAP, C), BF),
             pltpu.SemaphoreType.DMA((4, S)),
             pltpu.SemaphoreType.DMA((4, S)),
+            pltpu.VMEM((3, 2, 1024, C), BF),
+            pltpu.VMEM((3, 1024, C), BF),
+            pltpu.VMEM((3, 16, 64, C), BF),
+            pltpu.VMEM((3, 15, 64, C), BF),
+            pltpu.VMEM((3, 4, 64, C), F32),
+            pltpu.SemaphoreType.DMA((2, 3)),
+            pltpu.SemaphoreType.DMA((2, 3)),
+            pltpu.SemaphoreType.DMA((2, 3, 15)),
+            pltpu.SemaphoreType.DMA((2, 3, 15)),
+            pltpu.SemaphoreType.DMA((3, 3)),
+            pltpu.SemaphoreType.DMA((3, 3)),
         ],
         compiler_params=pltpu.CompilerParams(
             collective_id=0, has_side_effects=True, vmem_limit_bytes=56 * 2**20
         ),
     )(features, conv_weight, down_weight, neighbour_map, halo_rows, child_map, child_rows, out_grad)
-    conv_summed, down_summed = lax.psum((conv_terms, down_terms), "shard")
     grad_scale = 1.0 / math.sqrt(V * devices)
-    return (coarse, input_grad, conv_summed * grad_scale, down_summed * grad_scale)
+    return pl.pallas_call(
+        lambda *refs: finish(grad_scale, *refs),
+        out_shape=(
+            jax.ShapeDtypeStruct((PD, C2), BF),
+            jax.ShapeDtypeStruct((V, C), F32),
+            jax.ShapeDtypeStruct((K, C, C), F32),
+            jax.ShapeDtypeStruct((O, C, C2), F32),
+        ),
+        compiler_params=pltpu.CompilerParams(vmem_limit_bytes=60 * 2**20),
+    )(coarse, input_grad, summed)
 
 
 def solution(mesh):

time: 239 us -> 71.2 us (0.30)
  waiting for transfers between devices: 150 us -> 0 us
  between operations: 14 us -> 0.64 us
  other arithmetic: 4.07 us -> 0 us
    psum x1 -> x0, waiting for transfers between devices: 150 us -> none  [local(): conv_summed, down_summed = lax.psum((conv_terms, down_terms), 'shard')]
    mul x2 -> x0, other arithmetic: 4.07 us -> none  [the longest x1 3.01 us: local(): conv_summed * grad_scale]
    pallas_call x0 -> x1, Pallas kernels: none -> 3.42 us  [local(): pl.pallas_call(lambda *refs: finish(grad_scale, *refs), out_shape=(jax.Sh...]
  transfers between devices with their start and end apart: 1 -> 0, of which waited for: 1 -> 0; matrix products, arithmetic and copies ran while one was open for 0% -> 0% of each run, Pallas kernels for 0% -> 0%
where the time goes in v3:
time: 71.2 us; the launch traced here: 71.1 us
  Pallas kernels  70.4 us (99%)
    pallas_call x1, Pallas kernels, local(): pl.pallas_call(kernel, out_shape=(jax.ShapeDtypeStruct((PD, C2), BF), jax...  67 us
    pallas_call x1, Pallas kernels, local(): pl.pallas_call(lambda *refs: finish(grad_scale, *refs), out_shape=(jax.Sh...  3.42 us

profile of v3, /device:TPU:1, one launch (start us, length us, event | category | flops | bytes accessed | tf_op | source)
XLA Modules:
  0.0 71.1 jit_solution(10050428687864607996)
XLA Ops:
  0.6 67.0 %shard_map.111 = (bf16[256,256]{1,0:T(8,128)(2,1)}, f32[1024,128]{1,0:T(8,128)}, bf16[3,2048,128]{2,1,0:T(8,128)(2,1)}) custom-call(bf16[1024,128]{1,0:T(8,128)(2,1)} %features.1, bf16[27,128,128]{2,1,0:T(8,128)(2,1)} %conv_weight.1, bf16[8,128,256]{2,1,0:T(8,128)(2,1)} %down_weight.1, s32[27,1024]{1,0:T(8,128)} %neighbour_map.1, s32[4,64]{1,0:T(4,128)} %halo_rows.1, ...), custom_call_target="tpu_custom_call" | custom-call | tf_op jit(solution)/shard_map/pallas_call | solution.py:386
  67.6 3.4 %shard_map.112 = (bf16[256,256]{1,0:T(8,128)(2,1)}, f32[1024,128]{1,0:T(8,128)}, f32[27,128,128]{2,1,0:T(8,128)}, f32[8,128,256]{2,1,0:T(8,128)}) custom-call(bf16[256,256]{1,0:T(8,128)(2,1)} %get-tuple-element.7.refs_0_, f32[1024,128]{1,0:T(8,128)} %get-tuple-element.8.refs_1_, bf16[3,2048,128]{2,1,0:T(8,128)(2,1)} %get-tuple-element.9.refs_2_), custom_call_target="tpu_custom_call" | custom-call | tf_op jit(solution)/shard_map/pallas_call | solution.py:434

commit v4 on v3

v4 whole, which is shorter than its diff:
```python
import math

import jax
import jax.numpy as jnp
from jax import lax
from jax.experimental import pallas as pl
from jax.experimental.pallas import tpu as pltpu
from jax.sharding import PartitionSpec as P

MESH = pl.DeviceIdType.MESH
BF = jnp.bfloat16
F32 = jnp.float32
K = 27
O = 8
V = 1024
PD = 256
C = 128
C2 = 256
S = 4
CAP = 64
CAP2 = 32
HALF = V // 2
PAIRS = HALF + 128
OFFSETS = (-2, -1, 1, 2)
PLANES = ((2, 8, 32), (8, 32, 2), (32, 2, 8))
CHUNK = (64, 48, 64)
HOPS = [(i, j) for i in (2, 1, 3, 0) for j in (2, 1, 3, 0) if i or j]


def row_codes(rows, last, fold_received):
    received = rows >= V
    in_received = (rows >> 7) & 1 if fold_received else jnp.zeros_like(rows)
    side = jnp.where(received, in_received, (rows >> 9) & 1)
    block = jnp.where(received, 4, (rows >> 7) & 3)
    code = ((rows & 127) + 128) << block
    code = jnp.where(side == 1, -code, code)
    return jnp.where(rows >= last, 0, code).astype(F32)


def table_codes(shape, dim, start=0):
    place = lax.broadcasted_iota(jnp.int32, shape, dim) + start
    return (((place & 127) + 128) << (place >> 7)).astype(F32).astype(BF)


def pick_matrix(codes):
    size = jnp.abs(codes)
    names = table_codes((1, PAIRS), 1)
    one, zero = jnp.ones((), BF), jnp.zeros((), BF)
    return jnp.concatenate(
        [jnp.where(size == names[:, b * 128 : (b + 1) * 128], one, zero) for b in range(PAIRS // 128)], axis=1
    )


def spread_matrix(row, start, count):
    n = row.shape[1]
    size = jnp.broadcast_to(jnp.abs(row), (count, n)).astype(BF)
    names = table_codes((count, 128), 0, start)
    names = jnp.concatenate([names] * (n // 128), axis=1)
    return jnp.where(size == names, jnp.ones((), BF), jnp.zeros((), BF))


def pick_side(both, codes):
    both = both.astype(BF)
    return jnp.where(codes < 0, both[:, C:], both[:, :C])


def two_sides(rows, codes):
    zero = jnp.zeros((), BF)
    return jnp.concatenate([jnp.where(codes >= 0, rows, zero), jnp.where(codes < 0, rows, zero)], axis=1)


def dot(a, b):
    return jnp.dot(a, b, preferred_element_type=F32)


def dot_t(a, b):
    return lax.dot_general(a, b, (((1,), (1,)), ((), ())), preferred_element_type=F32)


def t_dot(a, b):
    return lax.dot_general(a, b, (((0,), (0,)), ((), ())), preferred_element_type=F32)


def unit_rows(rows, first, count):
    at = lax.broadcasted_iota(jnp.int32, (rows, 128 * count), 0)
    block = lax.broadcasted_iota(jnp.int32, (rows, 128 * count), 1) >> 7
    return (at == block + first).astype(F32).astype(BF)


def list_matrix(lists, cap):
    row = jnp.concatenate([lists[s : s + 1, :] for s in range(S)], axis=1)
    places = lax.broadcasted_iota(jnp.int32, (V, S * cap), 0)
    return (places == row).astype(F32).astype(BF)


def kernel(
    features_in, conv_weight_in, down_weight_in, neighbour_map_in, halo_rows_in, child_map_in, child_rows_in, out_grad_in,
    coarse, input_grad, summed,
    features, conv_weight, down_weight, neighbour_map, halo_rows, child_map, child_rows, out_grad, in_sems,
    codes_x, wide_x, wide_h, picked, table, pre, hidden, hidden_grad, pre_grad, z_all, back_x, spread_h,
    out_x, in_x, out_h, in_h, out_spread, in_spread, out_gx, in_gx, send_sem, recv_sem,
    terms, got_core, core_sum, got_plane, plane_sum,
    sum_send, sum_recv,
):
    n = lax.axis_size("shard")
    me = lax.axis_index("shard")
    core = lax.rem(me, 2)
    place = {stride: lax.rem(me // stride, 4) for stride in (2, 8, 32)}

    def shift(stride, by):
        return (lax.rem(place[stride] + by, 4) - place[stride]) * stride

    def device(by):
        return (lax.rem(me + by + n, n),)

    loads = [
        pltpu.make_async_copy(src, dst, in_sems.at[at])
        for at, (src, dst) in enumerate(
            (
                (halo_rows_in, halo_rows), (features_in, features), (neighbour_map_in, neighbour_map),
                (child_map_in, child_map), (out_grad_in, out_grad), (down_weight_in, down_weight),
                (conv_weight_in, conv_weight), (child_rows_in, child_rows),
            )
        )
    ]
    for load in loads:
        load.start()

    barrier = pltpu.get_barrier_semaphore()
    for by in OFFSETS:
        pl.semaphore_signal(barrier, inc=1, device_id=device(by), device_id_type=MESH)
    sibling = me + 1 - 2 * core
    pl.semaphore_signal(barrier, inc=1, device_id=(sibling,), device_id_type=MESH)
    for a, b, _ in PLANES:
        for i, j in HOPS:
            if i and j:
                to = me + shift(a, i) + shift(b, j)
                pl.semaphore_signal(barrier, inc=1, device_id=(to,), device_id_type=MESH)
        for i in (1, 2, 3):
            pl.semaphore_signal(barrier, inc=1, device_id=(me + shift(a, i),), device_id_type=MESH)

    def send(src, dst, sems, to):
        return pltpu.make_async_remote_copy(
            src_ref=src, dst_ref=dst, send_sem=sems[0], recv_sem=sems[1], device_id=(to,), device_id_type=MESH
        )

    flying = []

    def start_all(moves, whole, sems):
        for move in moves:
            move.start()
        group = send(whole, whole, sems, sibling)
        flying.append(group)
        return group

    def copies(which, src, dst, sign):
        sems = (send_sem.at[which], recv_sem.at[which])
        moves = [send(src.at[s], dst.at[s], sems, device(sign * OFFSETS[s])) for s in range(S)]
        return start_all(moves, src, sems)

    sums = [None] * 3

    def put_block(block, value):
        part = 0 if block < 16 else 1 if block < 28 else 2
        at = block - (0, 16, 28)[part]
        per_half = CHUNK[part] // 8
        terms[part, at // per_half, pl.ds(at % per_half * C, C), :] = value


    def sum_turn(turn, parts):
        for part in parts:
            if turn:
                sums[part].wait_recv()
            if turn < 5:
                sums[part] = sum_step(turn, part)

    def sum_step(turn, part):
        a, b, c = PLANES[part]
        size = CHUNK[part]
        here = place[a] * 4 + place[b]
        half = pl.ds(0, 16 * size)
        chunk = pl.ds(0, size)
        owned = pl.ds(pl.multiple_of(core * (16 * size) + here * size, 16), size)
        sems = (sum_send.at[turn, part], sum_recv.at[turn, part])
        fifteen = got_plane.at[part, :, chunk]
        if turn == 0:
            mine = terms.at[part, 1 - core, half]
            return start_all([send(mine, got_core.at[part, half], sems, sibling)], mine, sems)
        if turn == 1:
            total = (terms[part, core, half].astype(F32) + got_core[part, half].astype(F32)).astype(BF)
            for q in range(16):
                core_sum[part, q, chunk] = total[q * size : (q + 1) * size]
            moves = [
                send(
                    core_sum.at[part, lax.rem(place[a] + i, 4) * 4 + lax.rem(place[b] + j, 4), chunk],
                    got_plane.at[part, at, chunk], sems, me + shift(a, i) + shift(b, j),
                )
                for at, (i, j) in enumerate(HOPS)
            ]
            return start_all(moves, fifteen, sems)
        if turn == 2:
            total = core_sum[part, here, chunk].astype(F32)
            for at in range(15):
                total += got_plane[part, at, chunk].astype(F32)
            plane_sum[part, place[c], chunk] = total
            mine = plane_sum.at[part, place[c], chunk]
            moves = [send(mine, mine, sems, me + shift(c, i)) for i in (1, 2, 3)]
            return start_all(moves, plane_sum.at[part, pl.ds(0, 3), chunk], sems)
        if turn == 3:
            total = plane_sum[part, 0, chunk] + plane_sum[part, 1, chunk]
            total += plane_sum[part, 2, chunk] + plane_sum[part, 3, chunk]
            summed[part, owned] = total.astype(BF)
            mine = summed.at[part, owned]
            moves = [send(mine, mine, sems, me + shift(a, i) + shift(b, j)) for i, j in HOPS]
            return start_all(moves, fifteen, sems)
        mine = summed.at[part, pl.ds(pl.multiple_of(core * (16 * size), 16), 16 * size)]
        return start_all([send(mine, mine, sems, sibling)], mine, sems)

    loads[0].wait()
    loads[1].wait()
    chosen = t_dot(list_matrix(halo_rows[...], CAP), features[...]).astype(BF)
    for s in range(S):
        out_x[s] = chosen[s * CAP : (s + 1) * CAP]
    table[0:HALF, 0:C] = features[0:HALF, :]
    table[0:HALF, C : 2 * C] = features[HALF:V, :]

    loads[2].wait()
    codes_x[0:K, :] = row_codes(neighbour_map[...], V + S * CAP, True)
    codes_x[K:32, :] = jnp.zeros((32 - K, V), F32)
    turned_codes = codes_x[...].T.astype(BF)
    for k in range(0, K, 2):
        count = min(2, K - k)
        wide = dot(turned_codes, unit_rows(32, k, count)).astype(BF)
        for i in range(count):
            wide_x[k + i] = wide[:, i * 128 : (i + 1) * 128]
    pl.semaphore_wait(barrier, S + 37)
    send_x = copies(0, out_x, in_x, 1)

    for load in loads[3:]:
        load.wait()
    rows = child_map[...]
    plain = jnp.where(rows >= V + S * CAP2, 0, ((rows & 127) + 128) << (rows >> 7)).astype(F32)
    for o in range(O):
        total = dot(spread_matrix(plain[o : o + 1, :], 0, V + S * CAP2), out_grad[...]).astype(BF)
        spread_h[:, o * C2 : (o + 1) * C2] = total[0:V]
        for s in range(S):
            out_spread[s, :, o * C2 : (o + 1) * C2] = total[V + s * CAP2 : V + (s + 1) * CAP2]
    send_spread = copies(1, out_spread, in_spread, -1)
    total = jnp.zeros((V, C), F32)
    for o in range(O):
        total += dot_t(spread_h[:, o * C2 : (o + 1) * C2], down_weight[o])
    hidden_grad[...] = total
    send_x.wait_recv()
    for s in range(S):
        table[pl.ds(HALF + (s % 2) * CAP, CAP), pl.ds((s // 2) * C, C)] = in_x[s]
    pre[...] = jnp.zeros_like(pre)

    def forward(step, carry):
        k = step * 3
        group = []
        for i in range(3):
            codes = wide_x[k + i]
            rows = pick_side(dot(pick_matrix(codes), table[...]), codes)
            picked[k + i] = rows
            group.append(rows)
        weights = conv_weight[pl.ds(k, 3)].reshape(3 * C, C)
        pre[...] += dot(jnp.concatenate(group, axis=1), weights)
        return carry

    lax.fori_loop(0, K // 3, forward, 0)

    act = pre[...]
    gate = jax.nn.sigmoid(act)
    hidden[...] = (features[...].astype(F32) + act * gate).astype(BF)
    child_pick = list_matrix(child_rows[...], CAP2)
    chosen = t_dot(child_pick, hidden[...]).astype(BF)
    for s in range(S):
        out_h[s] = chosen[s * CAP2 : (s + 1) * CAP2]
    send_h = copies(2, out_h, in_h, 1)
    send_spread.wait_recv()
    turned_hidden = hidden[...].T
    turned_chosen = chosen.T
    for o in range(O):
        at = slice(o * C2, (o + 1) * C2)
        back_spread = jnp.concatenate([in_spread[s, :, at] for s in range(S)], axis=0)
        products = (dot(turned_hidden, spread_h[:, at]) + dot(turned_chosen, back_spread)).astype(BF)
        put_block(28 + 2 * o, products[:, 0:C])
        put_block(29 + 2 * o, products[:, C : 2 * C])
    sum_turn(0, (2,))

    returned = jnp.zeros((S * CAP2, C), F32)
    for o in range(O):
        back_spread = jnp.concatenate([in_spread[s, :, o * C2 : (o + 1) * C2] for s in range(S)], axis=0)
        returned += dot_t(back_spread, down_weight[o])
    grad_h = hidden_grad[...] + dot(child_pick, returned.astype(BF))
    hidden_grad[...] = grad_h
    pre_grad[...] = (grad_h * (gate * (1.0 + act * (1.0 - gate)))).astype(BF)

    turned_grad = pre_grad[...].T
    for k in range(0, K, 2):
        count = min(2, K - k)
        products = dot(turned_grad, jnp.concatenate([picked[k + i] for i in range(count)], axis=1))
        for i in range(count):
            put_block(k + i, products[:, i * C : (i + 1) * C].T.astype(BF))
        if k == 14:
            sum_turn(0, (0,))
    put_block(K, jnp.zeros((C, C), BF))
    sum_turn(0, (1,))
    sum_turn(1, (2,))
    sum_turn(1, (0,))

    back_x[...] = jnp.zeros_like(back_x)

    def backward(step, carry):
        k = step * 3
        z = dot_t(pre_grad[...], conv_weight[pl.ds(k, 3)].reshape(3 * C, C)).astype(BF)
        total = back_x[HALF:PAIRS, :]
        for i in range(3):
            z2 = two_sides(z[:, i * C : (i + 1) * C], wide_x[k + i])
            z_all[k + i] = z2
            total += dot(spread_matrix(codes_x[pl.ds(k + i, 1), :], HALF, 128), z2)
        back_x[HALF:PAIRS, :] = total
        return carry

    lax.fori_loop(0, 1, backward, 0)
    sum_turn(1, (1,))
    lax.fori_loop(1, 7, backward, 0)
    sum_turn(2, (2,))
    lax.fori_loop(7, 8, backward, 0)
    sum_turn(2, (0,))
    lax.fori_loop(8, K // 3, backward, 0)
    sum_turn(2, (1,))
    for s in range(S):
        out_gx[s] = back_x[pl.ds(HALF + (s % 2) * CAP, CAP), pl.ds((s // 2) * C, C)].astype(BF)
    send_gx = copies(3, out_gx, in_gx, -1)

    def backward_local(step, carry):
        k = step * 3
        total = back_x[0:HALF, :]
        for i in range(3):
            total += dot(spread_matrix(codes_x[pl.ds(k + i, 1), :], 0, HALF), z_all[k + i])
        back_x[0:HALF, :] = total
        return carry

    lax.fori_loop(0, 3, backward_local, 0)
    sum_turn(3, (2,))
    lax.fori_loop(3, 4, backward_local, 0)
    sum_turn(3, (0,))
    lax.fori_loop(4, 5, backward_local, 0)
    sum_turn(3, (1,))

    turned_codes = row_codes(child_map[...], V + S * CAP2, False).T.astype(BF)
    for o in range(0, O, 2):
        wide = dot(turned_codes, unit_rows(O, o, 2)).astype(BF)
        for i in range(2):
            wide_h[pl.ds((o + i) * PD, PD), :] = wide[:, i * 128 : (i + 1) * 128]
    table[0:HALF, 0:C] = hidden[0:HALF, :]
    table[0:HALF, C : 2 * C] = hidden[HALF:V, :]
    table[HALF:PAIRS, C : 2 * C] = jnp.zeros((128, C), BF)
    send_h.wait_recv()
    for s in range(S):
        table[pl.ds(HALF + s * CAP2, CAP2), 0:C] = in_h[s]
    total = jnp.zeros((PD, C2), F32)
    for o in range(O):
        codes = wide_h[pl.ds(o * PD, PD), :]
        rows = pick_side(dot(pick_matrix(codes), table[...]), codes)
        total += dot(rows, down_weight[o])
    coarse[...] = total.astype(BF)


    lax.fori_loop(5, K // 3, backward_local, 0)
    sum_turn(4, (2,))

    send_gx.wait_recv()
    returned = dot(list_matrix(halo_rows[...], CAP), jnp.concatenate([in_gx[s] for s in range(S)], axis=0))
    local_back = jnp.concatenate([back_x[0:HALF, 0:C], back_x[0:HALF, C : 2 * C]], axis=0)
    input_grad[...] = hidden_grad[...] + local_back + returned

    sum_turn(4, (0, 1))
    sum_turn(5, (0, 1, 2))
    for group in flying:
        group.wait_send()


FINISH = [(0, a, a + 4) for a in (0, 4, 8, 12)] + [(1, 0, 4), (1, 4, 8), (1, 8, 11)] + [(2, a, a + 4) for a in (0, 4, 8, 12)]


def finish(
    grad_scale, coarse_in, input_grad_in, summed_in, coarse, input_grad, conv_grad, down_grad,
    coarse_held, input_held, summed, conv_held, down_held, in_sems, out_sems,
):
    last = len(FINISH)
    loads = []
    for at, (part, first, end) in enumerate(FINISH):
        rows = pl.ds(first * C, (end - first) * C)
        loads.append(pltpu.make_async_copy(summed_in.at[part, rows], summed.at[part, rows], in_sems.at[at]))
    loads.append(pltpu.make_async_copy(coarse_in, coarse_held, in_sems.at[last]))
    loads.append(pltpu.make_async_copy(input_grad_in, input_held, in_sems.at[last + 1]))
    for load in loads:
        load.start()
    stores = []
    for at, (part, first, end) in enumerate(FINISH):
        loads[at].wait()
        for block in range(first, end):
            value = summed[part, block * C : (block + 1) * C, :].astype(F32) * grad_scale
            if part < 2:
                conv_held[part * 16 + block] = value
            else:
                down_held[block // 2, :, block % 2 * C : (block % 2 + 1) * C] = value
        if part < 2:
            held, out, rows = conv_held, conv_grad, pl.ds(part * 16 + first, end - first)
        else:
            held, out, rows = down_held, down_grad, pl.ds(first // 2, (end - first) // 2)
        stores.append(pltpu.make_async_copy(held.at[rows], out.at[rows], out_sems.at[at]))
        stores[-1].start()
    for at, (held, out) in enumerate(((coarse_held, coarse), (input_held, input_grad))):
        loads[last + at].wait()
        stores.append(pltpu.make_async_copy(held, out, out_sems.at[last + at]))
        stores[-1].start()
    for store in stores:
        store.wait()


def local(features, conv_weight, down_weight, neighbour_map, halo_rows, child_map, child_rows, out_grad):
    devices = lax.axis_size("shard")
    inputs = (features, conv_weight, down_weight, neighbour_map, halo_rows, child_map, child_rows, out_grad)
    coarse, input_grad, summed = pl.pallas_call(
        kernel,
        out_shape=(
            jax.ShapeDtypeStruct((PD, C2), BF),
            jax.ShapeDtypeStruct((V, C), F32),
            jax.ShapeDtypeStruct((3, 2048, C), BF),
        ),
        in_specs=[pl.BlockSpec(memory_space=pl.ANY)] * 8,
        scratch_shapes=[pltpu.VMEM(value.shape, value.dtype) for value in inputs] + [
            pltpu.SemaphoreType.DMA((8,)),
            pltpu.VMEM((32, V), F32),
            pltpu.VMEM((K, V, 128), BF),
            pltpu.VMEM((O * PD, 128), BF),
            pltpu.VMEM((K, V, C), BF),
            pltpu.VMEM((PAIRS, 2 * C), BF),
            pltpu.VMEM((V, C), F32),
            pltpu.VMEM((V, C), BF),
            pltpu.VMEM((V, C), F32),
            pltpu.VMEM((V, C), BF),
            pltpu.VMEM((K, V, 2 * C), BF),
            pltpu.VMEM((PAIRS, 2 * C), F32),
            pltpu.VMEM((V, O * C2), BF),
            pltpu.VMEM((S, CAP, C), BF),
            pltpu.VMEM((S, CAP, C), BF),
            pltpu.VMEM((S, CAP2, C), BF),
            pltpu.VMEM((S, CAP2, C), BF),
            pltpu.VMEM((S, CAP2, O * C2), BF),
            pltpu.VMEM((S, CAP2, O * C2), BF),
            pltpu.VMEM((S, CAP, C), BF),
            pltpu.VMEM((S, CAP, C), BF),
            pltpu.SemaphoreType.DMA((4,)),
            pltpu.SemaphoreType.DMA((4,)),
            pltpu.VMEM((3, 2, 1024, C), BF),
            pltpu.VMEM((3, 1024, C), BF),
            pltpu.VMEM((3, 16, 64, C), BF),
            pltpu.VMEM((3, 15, 64, C), BF),
            pltpu.VMEM((3, 4, 64, C), F32),
            pltpu.SemaphoreType.DMA((5, 3)),
            pltpu.SemaphoreType.DMA((5, 3)),
        ],
        compiler_params=pltpu.CompilerParams(
            collective_id=0, has_side_effects=True, vmem_limit_bytes=60 * 2**20
        ),
    )(*inputs)
    grad_scale = 1.0 / math.sqrt(V * devices)
    return pl.pallas_call(
        lambda *refs: finish(grad_scale, *refs),
        out_shape=(
            jax.ShapeDtypeStruct((PD, C2), BF),
            jax.ShapeDtypeStruct((V, C), F32),
            jax.ShapeDtypeStruct((K, C, C), F32),
            jax.ShapeDtypeStruct((O, C, C2), F32),
        ),
        in_specs=[pl.BlockSpec(memory_space=pl.ANY)] * 3,
        out_specs=[pl.BlockSpec(memory_space=pl.ANY)] * 4,
        scratch_shapes=[
            pltpu.VMEM((PD, C2), BF),
            pltpu.VMEM((V, C), F32),
            pltpu.VMEM((3, 2048, C), BF),
            pltpu.VMEM((K, C, C), F32),
            pltpu.VMEM((O, C, C2), F32),
            pltpu.SemaphoreType.DMA((len(FINISH) + 2,)),
            pltpu.SemaphoreType.DMA((len(FINISH) + 2,)),
        ],
        compiler_params=pltpu.CompilerParams(vmem_limit_bytes=60 * 2**20),
    )(coarse, input_grad, summed)


def solution(mesh):
    return jax.shard_map(
        local,
        mesh=mesh,
        in_specs=(
            P("shard", None),
            P(),
            P(),
            P(None, "shard"),
            P(None, "shard"),
            P(None, "shard"),
            P(None, "shard"),
            P("shard", None),
        ),
        out_specs=(P("shard", None), P("shard", None), P(), P()),
        check_vma=False,
    )
```

time: 71.2 us -> 64.5 us (0.906)
  Pallas kernels: 70.4 us -> 63.6 us
    pallas_call x1, Pallas kernels: 67 us -> 60.7 us  [local(): pl.pallas_call(kernel, out_shape=(jax.ShapeDtypeStruct((PD, C2), BF), jax...]
where the time goes in v4:
time: 64.5 us; the launch traced here: 64.4 us
  Pallas kernels  63.6 us (99%)
  between operations  0.8 us (1%)
    pallas_call x1, Pallas kernels, local(): pl.pallas_call(kernel, out_shape=(jax.ShapeDtypeStruct((PD, C2), BF), jax...  60.7 us
    pallas_call x1, Pallas kernels, local(): pl.pallas_call(lambda *refs: finish(grad_scale, *refs), out_shape=(jax.Sh...  2.92 us

profile of v4, /device:TPU:1, one launch (start us, length us, event | category | flops | bytes accessed | tf_op | source)
XLA Modules:
  0.0 64.4 jit_solution(1817466975510267909)
XLA Ops:
  0.6 60.7 %shard_map.111 = (bf16[256,256]{1,0:T(8,128)(2,1)}, f32[1024,128]{1,0:T(8,128)}, bf16[3,2048,128]{2,1,0:T(8,128)(2,1)}) custom-call(bf16[1024,128]{1,0:T(8,128)(2,1)} %features_in.1, bf16[27,128,128]{2,1,0:T(8,128)(2,1)} %conv_weight_in.1, bf16[8,128,256]{2,1,0:T(8,128)(2,1)} %down_weight_in.1, s32[27,1024]{1,0:T(8,128)} %neighbour_map_in.1, ...), custom_call_target="tpu_custom_call" | custom-call | tf_op jit(solution)/shard_map/pallas_call | solution.py:427
  61.3 2.9 %shard_map.112 = (bf16[256,256]{1,0:T(8,128)(2,1)}, f32[1024,128]{1,0:T(8,128)}, f32[27,128,128]{2,1,0:T(8,128)}, f32[8,128,256]{2,1,0:T(8,128)}) custom-call(bf16[256,256]{1,0:T(8,128)(2,1)} %get-tuple-element.7.refs_0_, f32[1024,128]{1,0:T(8,128)} %get-tuple-element.8.refs_1_, bf16[3,2048,128]{2,1,0:T(8,128)(2,1)} %get-tuple-element.9.refs_2_), custom_call_target="tpu_custom_call" | custom-call | tf_op jit(solution)/shard_map/pallas_call | solution.py:472

commit v5 on v4

--- a/solution.py
+++ b/solution.py
@@ -22,6 +22,7 @@
 HALF = V // 2
 PAIRS = HALF + 128
 OFFSETS = (-2, -1, 1, 2)
+EARLY = 2
 PLANES = ((2, 8, 32), (8, 32, 2), (32, 2, 8))
 CHUNK = (64, 48, 64)
 HOPS = [(i, j) for i in (2, 1, 3, 0) for j in (2, 1, 3, 0) if i or j]
@@ -42,12 +43,12 @@
     return (((place & 127) + 128) << (place >> 7)).astype(F32).astype(BF)
 
 
-def pick_matrix(codes):
+def pick_matrix(codes, first=0, end=PAIRS // 128):
     size = jnp.abs(codes)
     names = table_codes((1, PAIRS), 1)
     one, zero = jnp.ones((), BF), jnp.zeros((), BF)
     return jnp.concatenate(
-        [jnp.where(size == names[:, b * 128 : (b + 1) * 128], one, zero) for b in range(PAIRS // 128)], axis=1
+        [jnp.where(size == names[:, b * 128 : (b + 1) * 128], one, zero) for b in range(first, end)], axis=1
     )
 
 
@@ -95,7 +96,8 @@
 
 def kernel(
     features_in, conv_weight_in, down_weight_in, neighbour_map_in, halo_rows_in, child_map_in, child_rows_in, out_grad_in,
-    coarse, input_grad, summed,
+    coarse_out, input_grad_out, summed_out,
+    coarse, input_grad, summed, out_sems,
     features, conv_weight, down_weight, neighbour_map, halo_rows, child_map, child_rows, out_grad, in_sems,
     codes_x, wide_x, wide_h, picked, table, pre, hidden, hidden_grad, pre_grad, z_all, back_x, spread_h,
     out_x, in_x, out_h, in_h, out_spread, in_spread, out_gx, in_gx, send_sem, recv_sem,
@@ -125,6 +127,11 @@
     ]
     for load in loads:
         load.start()
+
+    results = [
+        pltpu.make_async_copy(coarse, coarse_out, out_sems.at[0]),
+        pltpu.make_async_copy(input_grad, input_grad_out, out_sems.at[1]),
+    ] + [pltpu.make_async_copy(summed.at[part], summed_out.at[part], out_sems.at[2 + part]) for part in range(3)]
 
     barrier = pltpu.get_barrier_semaphore()
     for by in OFFSETS:
@@ -250,24 +257,48 @@
     for o in range(O):
         total += dot_t(spread_h[:, o * C2 : (o + 1) * C2], down_weight[o])
     hidden_grad[...] = total
+    def pick_local(step, carry):
+        for i in range(3):
+            k = step * 3 + i
+            z_all[k] = dot(pick_matrix(wide_x[k], 0, 4), table[0:HALF, :]).astype(BF)
+        return carry
+
+    lax.fori_loop(0, EARLY, pick_local, 0)
     send_x.wait_recv()
     for s in range(S):
         table[pl.ds(HALF + (s % 2) * CAP, CAP), pl.ds((s // 2) * C, C)] = in_x[s]
     pre[...] = jnp.zeros_like(pre)
 
-    def forward(step, carry):
-        k = step * 3
+    def multiply(k, group):
+        weights = conv_weight[pl.ds(k, len(group))].reshape(len(group) * C, C)
+        pre[...] += dot(jnp.concatenate(group, axis=1), weights)
+
+    def forward_early(step, carry):
         group = []
         for i in range(3):
-            codes = wide_x[k + i]
+            k = step * 3 + i
+            codes = wide_x[k]
+            both = dot(pick_matrix(codes, 4, 5), table[HALF:PAIRS, :]).astype(BF) + z_all[k]
+            rows = jnp.where(codes < 0, both[:, C:], both[:, :C])
+            picked[k] = rows
+            group.append(rows)
+        multiply(step * 3, group)
+        return carry
+
+    lax.fori_loop(0, EARLY, forward_early, 0)
+
+    def forward(step, carry):
+        group = []
+        for i in range(3):
+            k = step * 3 + i
+            codes = wide_x[k]
             rows = pick_side(dot(pick_matrix(codes), table[...]), codes)
-            picked[k + i] = rows
+            picked[k] = rows
             group.append(rows)
-        weights = conv_weight[pl.ds(k, 3)].reshape(3 * C, C)
-        pre[...] += dot(jnp.concatenate(group, axis=1), weights)
+        multiply(step * 3, group)
         return carry
 
-    lax.fori_loop(0, K // 3, forward, 0)
+    lax.fori_loop(EARLY, K // 3, forward, 0)
 
     act = pre[...]
     gate = jax.nn.sigmoid(act)
@@ -304,9 +335,9 @@
             put_block(k + i, products[:, i * C : (i + 1) * C].T.astype(BF))
         if k == 14:
             sum_turn(0, (0,))
+            sum_turn(1, (2,))
     put_block(K, jnp.zeros((C, C), BF))
     sum_turn(0, (1,))
-    sum_turn(1, (2,))
     sum_turn(1, (0,))
 
     back_x[...] = jnp.zeros_like(back_x)
@@ -324,12 +355,7 @@
 
     lax.fori_loop(0, 1, backward, 0)
     sum_turn(1, (1,))
-    lax.fori_loop(1, 7, backward, 0)
-    sum_turn(2, (2,))
-    lax.fori_loop(7, 8, backward, 0)
-    sum_turn(2, (0,))
-    lax.fori_loop(8, K // 3, backward, 0)
-    sum_turn(2, (1,))
+    lax.fori_loop(1, K // 3, backward, 0)
     for s in range(S):
         out_gx[s] = back_x[pl.ds(HALF + (s % 2) * CAP, CAP), pl.ds((s // 2) * C, C)].astype(BF)
     send_gx = copies(3, out_gx, in_gx, -1)
@@ -342,12 +368,9 @@
         back_x[0:HALF, :] = total
         return carry
 
-    lax.fori_loop(0, 3, backward_local, 0)
-    sum_turn(3, (2,))
-    lax.fori_loop(3, 4, backward_local, 0)
-    sum_turn(3, (0,))
-    lax.fori_loop(4, 5, backward_local, 0)
-    sum_turn(3, (1,))
+    sum_turn(2, (2, 0, 1))
+    lax.fori_loop(0, 4, backward_local, 0)
+    sum_turn(3, (2, 0, 1))
 
     turned_codes = row_codes(child_map[...], V + S * CAP2, False).T.astype(BF)
     for o in range(0, O, 2):
@@ -366,18 +389,23 @@
         rows = pick_side(dot(pick_matrix(codes), table[...]), codes)
         total += dot(rows, down_weight[o])
     coarse[...] = total.astype(BF)
-
-
-    lax.fori_loop(5, K // 3, backward_local, 0)
-    sum_turn(4, (2,))
+    results[0].start()
+
+
+    lax.fori_loop(4, K // 3, backward_local, 0)
 
     send_gx.wait_recv()
     returned = dot(list_matrix(halo_rows[...], CAP), jnp.concatenate([in_gx[s] for s in range(S)], axis=0))
     local_back = jnp.concatenate([back_x[0:HALF, 0:C], back_x[0:HALF, C : 2 * C]], axis=0)
     input_grad[...] = hidden_grad[...] + local_back + returned
 
-    sum_turn(4, (0, 1))
-    sum_turn(5, (0, 1, 2))
+    results[1].start()
+    sum_turn(4, (2, 0, 1))
+    for part in (2, 0, 1):
+        sum_turn(5, (part,))
+        results[2 + part].start()
+    for result in results:
+        result.wait()
     for group in flying:
         group.wait_send()
 
@@ -432,7 +460,13 @@
             jax.ShapeDtypeStruct((3, 2048, C), BF),
         ),
         in_specs=[pl.BlockSpec(memory_space=pl.ANY)] * 8,
-        scratch_shapes=[pltpu.VMEM(value.shape, value.dtype) for value in inputs] + [
+        out_specs=[pl.BlockSpec(memory_space=pl.ANY)] * 3,
+        scratch_shapes=[
+            pltpu.VMEM((PD, C2), BF),
+            pltpu.VMEM((V, C), F32),
+            pltpu.VMEM((3, 2048, C), BF),
+            pltpu.SemaphoreType.DMA((5,)),
+        ] + [pltpu.VMEM(value.shape, value.dtype) for value in inputs] + [
             pltpu.SemaphoreType.DMA((8,)),
             pltpu.VMEM((32, V), F32),
             pltpu.VMEM((K, V, 128), BF),

time: 64.5 us -> 62.1 us (0.963)
  Pallas kernels: 63.6 us -> 61.1 us
    pallas_call x1, Pallas kernels: 60.7 us -> 58.2 us  [local(): pl.pallas_call(kernel, out_shape=(jax.ShapeDtypeStruct((PD, C2), BF), jax...]
where the time goes in v5:
time: 62.1 us; the launch traced here: 61.9 us
  Pallas kernels  61.1 us (98%)
  between operations  0.8 us (1%)
    pallas_call x1, Pallas kernels, local(): pl.pallas_call(kernel, out_shape=(jax.ShapeDtypeStruct((PD, C2), BF), jax...  58.2 us
    pallas_call x1, Pallas kernels, local(): pl.pallas_call(lambda *refs: finish(grad_scale, *refs), out_shape=(jax.Sh...  2.92 us

profile of v5, /device:TPU:1, one launch (start us, length us, event | category | flops | bytes accessed | tf_op | source)
XLA Modules:
  0.0 61.9 jit_solution(13084098313967616347)
XLA Ops:
  0.6 58.2 %shard_map.111 = (bf16[256,256]{1,0:T(8,128)(2,1)}, f32[1024,128]{1,0:T(8,128)}, bf16[3,2048,128]{2,1,0:T(8,128)(2,1)}) custom-call(bf16[1024,128]{1,0:T(8,128)(2,1)} %features_in.1, bf16[27,128,128]{2,1,0:T(8,128)(2,1)} %conv_weight_in.1, bf16[8,128,256]{2,1,0:T(8,128)(2,1)} %down_weight_in.1, s32[27,1024]{1,0:T(8,128)} %neighbour_map_in.1, ...), custom_call_target="tpu_custom_call" | custom-call | tf_op jit(solution)/shard_map/pallas_call | solution.py:455
  58.8 2.9 %shard_map.112 = (bf16[256,256]{1,0:T(8,128)(2,1)}, f32[1024,128]{1,0:T(8,128)}, f32[27,128,128]{2,1,0:T(8,128)}, f32[8,128,256]{2,1,0:T(8,128)}) custom-call(bf16[256,256]{1,0:T(8,128)(2,1)} %get-tuple-element.7.refs_0_, f32[1024,128]{1,0:T(8,128)} %get-tuple-element.8.refs_1_, bf16[3,2048,128]{2,1,0:T(8,128)(2,1)} %get-tuple-element.9.refs_2_), custom_call_target="tpu_custom_call" | custom-call | tf_op jit(solution)/shard_map/pallas_call | solution.py:506

commit v6 on v5

--- a/solution.py
+++ b/solution.py
@@ -11,6 +11,8 @@
 BF = jnp.bfloat16
 F32 = jnp.float32
 K = 27
+SELF = 13
+G = K - 1
 O = 8
 V = 1024
 PD = 256
@@ -22,6 +24,7 @@
 HALF = V // 2
 PAIRS = HALF + 128
 OFFSETS = (-2, -1, 1, 2)
+LOCAL_FIRST = 3
 EARLY = 2
 PLANES = ((2, 8, 32), (8, 32, 2), (32, 2, 8))
 CHUNK = (64, 48, 64)
@@ -96,8 +99,7 @@
 
 def kernel(
     features_in, conv_weight_in, down_weight_in, neighbour_map_in, halo_rows_in, child_map_in, child_rows_in, out_grad_in,
-    coarse_out, input_grad_out, summed_out,
-    coarse, input_grad, summed, out_sems,
+    coarse, input_grad, summed,
     features, conv_weight, down_weight, neighbour_map, halo_rows, child_map, child_rows, out_grad, in_sems,
     codes_x, wide_x, wide_h, picked, table, pre, hidden, hidden_grad, pre_grad, z_all, back_x, spread_h,
     out_x, in_x, out_h, in_h, out_spread, in_spread, out_gx, in_gx, send_sem, recv_sem,
@@ -121,17 +123,15 @@
             (
                 (halo_rows_in, halo_rows), (features_in, features), (neighbour_map_in, neighbour_map),
                 (child_map_in, child_map), (out_grad_in, out_grad), (down_weight_in, down_weight),
-                (conv_weight_in, conv_weight), (child_rows_in, child_rows),
+                (child_rows_in, child_rows),
+                (conv_weight_in.at[pl.ds(0, SELF)], conv_weight.at[pl.ds(0, SELF)]),
+                (conv_weight_in.at[pl.ds(SELF + 1, G - SELF - 1)], conv_weight.at[pl.ds(SELF + 1, G - SELF - 1)]),
+                (conv_weight_in.at[G], conv_weight.at[SELF]), (conv_weight_in.at[SELF], conv_weight.at[G]),
             )
         )
     ]
     for load in loads:
         load.start()
-
-    results = [
-        pltpu.make_async_copy(coarse, coarse_out, out_sems.at[0]),
-        pltpu.make_async_copy(input_grad, input_grad_out, out_sems.at[1]),
-    ] + [pltpu.make_async_copy(summed.at[part], summed_out.at[part], out_sems.at[2 + part]) for part in range(3)]
 
     barrier = pltpu.get_barrier_semaphore()
     for by in OFFSETS:
@@ -232,13 +232,14 @@
     table[0:HALF, C : 2 * C] = features[HALF:V, :]
 
     loads[2].wait()
-    codes_x[0:K, :] = row_codes(neighbour_map[...], V + S * CAP, True)
-    codes_x[K:32, :] = jnp.zeros((32 - K, V), F32)
+    codes = row_codes(neighbour_map[...], V + S * CAP, True)
+    codes_x[0:K, :] = codes
+    codes_x[SELF : SELF + 1, :] = codes[G:K, :]
+    codes_x[G:32, :] = jnp.zeros((32 - G, V), F32)
     turned_codes = codes_x[...].T.astype(BF)
-    for k in range(0, K, 2):
-        count = min(2, K - k)
-        wide = dot(turned_codes, unit_rows(32, k, count)).astype(BF)
-        for i in range(count):
+    for k in range(0, G, 2):
+        wide = dot(turned_codes, unit_rows(32, k, 2)).astype(BF)
+        for i in range(2):
             wide_x[k + i] = wide[:, i * 128 : (i + 1) * 128]
     pl.semaphore_wait(barrier, S + 37)
     send_x = copies(0, out_x, in_x, 1)
@@ -264,10 +265,10 @@
         return carry
 
     lax.fori_loop(0, EARLY, pick_local, 0)
+    pre[...] = dot(features[...], conv_weight[G])
     send_x.wait_recv()
     for s in range(S):
         table[pl.ds(HALF + (s % 2) * CAP, CAP), pl.ds((s // 2) * C, C)] = in_x[s]
-    pre[...] = jnp.zeros_like(pre)
 
     def multiply(k, group):
         weights = conv_weight[pl.ds(k, len(group))].reshape(len(group) * C, C)
@@ -288,17 +289,17 @@
     lax.fori_loop(0, EARLY, forward_early, 0)
 
     def forward(step, carry):
+        first = EARLY * 3 + step * 4
         group = []
-        for i in range(3):
-            k = step * 3 + i
-            codes = wide_x[k]
+        for i in range(4):
+            codes = wide_x[first + i]
             rows = pick_side(dot(pick_matrix(codes), table[...]), codes)
-            picked[k] = rows
+            picked[first + i] = rows
             group.append(rows)
-        multiply(step * 3, group)
+        multiply(first, group)
         return carry
 
-    lax.fori_loop(EARLY, K // 3, forward, 0)
+    lax.fori_loop(0, (G - EARLY * 3) // 4, forward, 0)
 
     act = pre[...]
     gate = jax.nn.sigmoid(act)
@@ -328,11 +329,11 @@
     pre_grad[...] = (grad_h * (gate * (1.0 + act * (1.0 - gate)))).astype(BF)
 
     turned_grad = pre_grad[...].T
-    for k in range(0, K, 2):
-        count = min(2, K - k)
-        products = dot(turned_grad, jnp.concatenate([picked[k + i] for i in range(count)], axis=1))
-        for i in range(count):
-            put_block(k + i, products[:, i * C : (i + 1) * C].T.astype(BF))
+    put_block(SELF, t_dot(features[...], pre_grad[...]).astype(BF))
+    for k in range(0, G, 2):
+        products = dot(turned_grad, jnp.concatenate([picked[k], picked[k + 1]], axis=1))
+        for i in range(2):
+            put_block(G if k + i == SELF else k + i, products[:, i * C : (i + 1) * C].T.astype(BF))
         if k == 14:
             sum_turn(0, (0,))
             sum_turn(1, (2,))
@@ -342,34 +343,39 @@
 
     back_x[...] = jnp.zeros_like(back_x)
 
+    def backward_group(first, count):
+        weights = conv_weight[pl.ds(first, count)].reshape(count * C, C)
+        z = dot_t(pre_grad[...], weights).astype(BF)
+        total = back_x[HALF:PAIRS, :]
+        for i in range(count):
+            z2 = two_sides(z[:, i * C : (i + 1) * C], wide_x[first + i])
+            z_all[first + i] = z2
+            total += dot(spread_matrix(codes_x[pl.ds(first + i, 1), :], HALF, 128), z2)
+        back_x[HALF:PAIRS, :] = total
+
     def backward(step, carry):
-        k = step * 3
-        z = dot_t(pre_grad[...], conv_weight[pl.ds(k, 3)].reshape(3 * C, C)).astype(BF)
-        total = back_x[HALF:PAIRS, :]
-        for i in range(3):
-            z2 = two_sides(z[:, i * C : (i + 1) * C], wide_x[k + i])
-            z_all[k + i] = z2
-            total += dot(spread_matrix(codes_x[pl.ds(k + i, 1), :], HALF, 128), z2)
-        back_x[HALF:PAIRS, :] = total
+        backward_group(step * 4, 4)
         return carry
 
-    lax.fori_loop(0, 1, backward, 0)
+    backward_group(G - 2, 2)
     sum_turn(1, (1,))
-    lax.fori_loop(1, K // 3, backward, 0)
+    lax.fori_loop(0, G // 4, backward, 0)
     for s in range(S):
         out_gx[s] = back_x[pl.ds(HALF + (s % 2) * CAP, CAP), pl.ds((s // 2) * C, C)].astype(BF)
     send_gx = copies(3, out_gx, in_gx, -1)
 
+    def backward_local_group(first, count):
+        total = back_x[0:HALF, :]
+        for i in range(count):
+            total += dot(spread_matrix(codes_x[pl.ds(first + i, 1), :], 0, HALF), z_all[first + i])
+        back_x[0:HALF, :] = total
+
     def backward_local(step, carry):
-        k = step * 3
-        total = back_x[0:HALF, :]
-        for i in range(3):
-            total += dot(spread_matrix(codes_x[pl.ds(k + i, 1), :], 0, HALF), z_all[k + i])
-        back_x[0:HALF, :] = total
+        backward_local_group(step * 4, 4)
         return carry
 
     sum_turn(2, (2, 0, 1))
-    lax.fori_loop(0, 4, backward_local, 0)
+    lax.fori_loop(0, LOCAL_FIRST, backward_local, 0)
     sum_turn(3, (2, 0, 1))
 
     turned_codes = row_codes(child_map[...], V + S * CAP2, False).T.astype(BF)
@@ -389,23 +395,19 @@
         rows = pick_side(dot(pick_matrix(codes), table[...]), codes)
         total += dot(rows, down_weight[o])
     coarse[...] = total.astype(BF)
-    results[0].start()
-
-
-    lax.fori_loop(4, K // 3, backward_local, 0)
+
+
+    lax.fori_loop(LOCAL_FIRST, G // 4, backward_local, 0)
+    backward_local_group(G - 2, 2)
+    hidden_grad[...] += dot_t(pre_grad[...], conv_weight[G])
 
     send_gx.wait_recv()
     returned = dot(list_matrix(halo_rows[...], CAP), jnp.concatenate([in_gx[s] for s in range(S)], axis=0))
     local_back = jnp.concatenate([back_x[0:HALF, 0:C], back_x[0:HALF, C : 2 * C]], axis=0)
     input_grad[...] = hidden_grad[...] + local_back + returned
 
-    results[1].start()
     sum_turn(4, (2, 0, 1))
-    for part in (2, 0, 1):
-        sum_turn(5, (part,))
-        results[2 + part].start()
-    for result in results:
-        result.wait()
+    sum_turn(5, (2, 0, 1))
     for group in flying:
         group.wait_send()
 
@@ -414,21 +416,17 @@
 
 
 def finish(
-    grad_scale, coarse_in, input_grad_in, summed_in, coarse, input_grad, conv_grad, down_grad,
-    coarse_held, input_held, summed, conv_held, down_held, in_sems, out_sems,
+    grad_scale, coarse_in, input_grad_in, summed, coarse, input_grad, conv_grad, down_grad, conv_held, down_held, out_sems
 ):
-    last = len(FINISH)
-    loads = []
-    for at, (part, first, end) in enumerate(FINISH):
-        rows = pl.ds(first * C, (end - first) * C)
-        loads.append(pltpu.make_async_copy(summed_in.at[part, rows], summed.at[part, rows], in_sems.at[at]))
-    loads.append(pltpu.make_async_copy(coarse_in, coarse_held, in_sems.at[last]))
-    loads.append(pltpu.make_async_copy(input_grad_in, input_held, in_sems.at[last + 1]))
-    for load in loads:
-        load.start()
     stores = []
-    for at, (part, first, end) in enumerate(FINISH):
-        loads[at].wait()
+
+    def store(held, out):
+        stores.append(pltpu.make_async_copy(held, out, out_sems.at[len(stores)]))
+        stores[-1].start()
+
+    store(input_grad_in, input_grad)
+    store(coarse_in, coarse)
+    for part, first, end in FINISH:
         for block in range(first, end):
             value = summed[part, block * C : (block + 1) * C, :].astype(F32) * grad_scale
             if part < 2:
@@ -436,17 +434,13 @@
             else:
                 down_held[block // 2, :, block % 2 * C : (block % 2 + 1) * C] = value
         if part < 2:
-            held, out, rows = conv_held, conv_grad, pl.ds(part * 16 + first, end - first)
+            rows = pl.ds(part * 16 + first, end - first)
+            store(conv_held.at[rows], conv_grad.at[rows])
         else:
-            held, out, rows = down_held, down_grad, pl.ds(first // 2, (end - first) // 2)
-        stores.append(pltpu.make_async_copy(held.at[rows], out.at[rows], out_sems.at[at]))
-        stores[-1].start()
-    for at, (held, out) in enumerate(((coarse_held, coarse), (input_held, input_grad))):
-        loads[last + at].wait()
-        stores.append(pltpu.make_async_copy(held, out, out_sems.at[last + at]))
-        stores[-1].start()
-    for store in stores:
-        store.wait()
+            rows = pl.ds(first // 2, (end - first) // 2)
+            store(down_held.at[rows], down_grad.at[rows])
+    for copy in stores:
+        copy.wait()
 
 
 def local(features, conv_weight, down_weight, neighbour_map, halo_rows, child_map, child_rows, out_grad):
@@ -455,29 +449,24 @@
     coarse, input_grad, summed = pl.pallas_call(
         kernel,
         out_shape=(
-            jax.ShapeDtypeStruct((PD, C2), BF),
-            jax.ShapeDtypeStruct((V, C), F32),
-            jax.ShapeDtypeStruct((3, 2048, C), BF),
-        ),
-        in_specs=[pl.BlockSpec(memory_space=pl.ANY)] * 8,
-        out_specs=[pl.BlockSpec(memory_space=pl.ANY)] * 3,
-        scratch_shapes=[
             pltpu.VMEM((PD, C2), BF),
             pltpu.VMEM((V, C), F32),
             pltpu.VMEM((3, 2048, C), BF),
-            pltpu.SemaphoreType.DMA((5,)),
-        ] + [pltpu.VMEM(value.shape, value.dtype) for value in inputs] + [
-            pltpu.SemaphoreType.DMA((8,)),
+        ),
+        in_specs=[pl.BlockSpec(memory_space=pl.ANY)] * 8,
+        out_specs=[pl.BlockSpec(memory_space=pltpu.VMEM)] * 3,
+        scratch_shapes=[pltpu.VMEM(value.shape, value.dtype) for value in inputs] + [
+            pltpu.SemaphoreType.DMA((11,)),
             pltpu.VMEM((32, V), F32),
-            pltpu.VMEM((K, V, 128), BF),
+            pltpu.VMEM((G, V, 128), BF),
             pltpu.VMEM((O * PD, 128), BF),
-            pltpu.VMEM((K, V, C), BF),
+            pltpu.VMEM((G, V, C), BF),
             pltpu.VMEM((PAIRS, 2 * C), BF),
             pltpu.VMEM((V, C), F32),
             pltpu.VMEM((V, C), BF),
             pltpu.VMEM((V, C), F32),
             pltpu.VMEM((V, C), BF),
-            pltpu.VMEM((K, V, 2 * C), BF),
+            pltpu.VMEM((G, V, 2 * C), BF),
             pltpu.VMEM((PAIRS, 2 * C), F32),
             pltpu.VMEM((V, O * C2), BF),
             pltpu.VMEM((S, CAP, C), BF),
@@ -499,7 +488,7 @@
             pltpu.SemaphoreType.DMA((5, 3)),
         ],
         compiler_params=pltpu.CompilerParams(
-            collective_id=0, has_side_effects=True, vmem_limit_bytes=60 * 2**20
+            collective_id=0, has_side_effects=True, vmem_limit_bytes=52 * 2**20
         ),
     )(*inputs)
     grad_scale = 1.0 / math.sqrt(V * devices)
@@ -511,19 +500,15 @@
             jax.ShapeDtypeStruct((K, C, C), F32),
             jax.ShapeDtypeStruct((O, C, C2), F32),
         ),
-        in_specs=[pl.BlockSpec(memory_space=pl.ANY)] * 3,
+        in_specs=[pl.BlockSpec(memory_space=pltpu.VMEM)] * 3,
         out_specs=[pl.BlockSpec(memory_space=pl.ANY)] * 4,
         scratch_shapes=[
-            pltpu.VMEM((PD, C2), BF),
-            pltpu.VMEM((V, C), F32),
-            pltpu.VMEM((3, 2048, C), BF),
             pltpu.VMEM((K, C, C), F32),
             pltpu.VMEM((O, C, C2), F32),
             pltpu.SemaphoreType.DMA((len(FINISH) + 2,)),
-            pltpu.SemaphoreType.DMA((len(FINISH) + 2,)),
         ],
-        compiler_params=pltpu.CompilerParams(vmem_limit_bytes=60 * 2**20),
-    )(coarse, input_grad, summed)
+        compiler_params=pltpu.CompilerParams(vmem_limit_bytes=52 * 2**20),
+    )(*[pltpu.with_memory_space_constraint(value, pltpu.VMEM) for value in (coarse, input_grad, summed)])
 
 
 def solution(mesh):

time: 62.1 us -> 58 us (0.934)
  Pallas kernels: 61.1 us -> 57.1 us
    pallas_call x1, Pallas kernels: 58.2 us -> 55.2 us  [local(): pl.pallas_call(kernel, out_shape=(pltpu.VMEM((PD, C2), BF), pltpu.VMEM((V...]
    pallas_call x1, Pallas kernels: 2.92 us -> 1.87 us  [local(): pl.pallas_call(lambda *refs: finish(grad_scale, *refs), out_shape=(jax.Sh...]
where the time goes in v6:
time: 58 us; the launch traced here: 57.9 us
  Pallas kernels  57.1 us (98%)
  between operations  0.8 us (1%)
    pallas_call x1, Pallas kernels, local(): pl.pallas_call(kernel, out_shape=(pltpu.VMEM((PD, C2), BF), pltpu.VMEM((V...  55.2 us
    pallas_call x1, Pallas kernels, local(): pl.pallas_call(lambda *refs: finish(grad_scale, *refs), out_shape=(jax.Sh...  1.87 us

profile of v6, /device:TPU:1, one launch (start us, length us, event | category | flops | bytes accessed | tf_op | source)
XLA Modules:
  0.0 57.9 jit_solution(6783670665957007344)
XLA Ops:
  0.6 55.2 %shard_map.111 = (bf16[256,256]{1,0:T(8,128)(2,1)S(1)}, f32[1024,128]{1,0:T(8,128)S(1)}, bf16[3,2048,128]{2,1,0:T(8,128)(2,1)S(1)}) custom-call(bf16[1024,128]{1,0:T(8,128)(2,1)} %features_in.1, bf16[27,128,128]{2,1,0:T(8,128)(2,1)} %conv_weight_in.1, bf16[8,128,256]{2,1,0:T(8,128)(2,1)} %down_weight_in.1, s32[27,1024]{1,0:T(8,128)} %neighbour_map_in.1, ...), custom_call_target="tpu_custom_call" | custom-call | tf_op jit(solution)/shard_map/pallas_call | solution.py:449
  55.8 1.9 %shard_map.112 = (bf16[256,256]{1,0:T(8,128)(2,1)}, f32[1024,128]{1,0:T(8,128)}, f32[27,128,128]{2,1,0:T(8,128)}, f32[8,128,256]{2,1,0:T(8,128)}) custom-call(bf16[256,256]{1,0:T(8,128)(2,1)S(1)} %get-tuple-element.7.refs_0_, f32[1024,128]{1,0:T(8,128)S(1)} %get-tuple-element.8.refs_1_, bf16[3,2048,128]{2,1,0:T(8,128)(2,1)S(1)} %get-tuple-element.9.refs_2_), custom_call_target="tpu_custom_call" | custom-call | tf_op jit(solution)/shard_map/pallas_call | solution.py:495

commit v7 on v6

--- a/solution.py
+++ b/solution.py
@@ -25,7 +25,7 @@
 PAIRS = HALF + 128
 OFFSETS = (-2, -1, 1, 2)
 LOCAL_FIRST = 3
-EARLY = 2
+EARLY = 1
 PLANES = ((2, 8, 32), (8, 32, 2), (32, 2, 8))
 CHUNK = (64, 48, 64)
 HOPS = [(i, j) for i in (2, 1, 3, 0) for j in (2, 1, 3, 0) if i or j]
@@ -259,8 +259,8 @@
         total += dot_t(spread_h[:, o * C2 : (o + 1) * C2], down_weight[o])
     hidden_grad[...] = total
     def pick_local(step, carry):
-        for i in range(3):
-            k = step * 3 + i
+        for i in range(2):
+            k = step * 2 + i
             z_all[k] = dot(pick_matrix(wide_x[k], 0, 4), table[0:HALF, :]).astype(BF)
         return carry
 
@@ -276,22 +276,22 @@
 
     def forward_early(step, carry):
         group = []
-        for i in range(3):
-            k = step * 3 + i
+        for i in range(2):
+            k = step * 2 + i
             codes = wide_x[k]
             both = dot(pick_matrix(codes, 4, 5), table[HALF:PAIRS, :]).astype(BF) + z_all[k]
             rows = jnp.where(codes < 0, both[:, C:], both[:, :C])
             picked[k] = rows
             group.append(rows)
-        multiply(step * 3, group)
+        multiply(step * 2, group)
         return carry
 
     lax.fori_loop(0, EARLY, forward_early, 0)
 
     def forward(step, carry):
-        first = EARLY * 3 + step * 4
+        first = EARLY * 2 + step * 6
         group = []
-        for i in range(4):
+        for i in range(6):
             codes = wide_x[first + i]
             rows = pick_side(dot(pick_matrix(codes), table[...]), codes)
             picked[first + i] = rows
@@ -299,7 +299,7 @@
         multiply(first, group)
         return carry
 
-    lax.fori_loop(0, (G - EARLY * 3) // 4, forward, 0)
+    lax.fori_loop(0, (G - EARLY * 2) // 6, forward, 0)
 
     act = pre[...]
     gate = jax.nn.sigmoid(act)

time: 58 us -> 56.6 us (0.976)
  Pallas kernels: 57.1 us -> 55.6 us
    pallas_call x1, Pallas kernels: 55.2 us -> 53.8 us  [local(): pl.pallas_call(kernel, out_shape=(pltpu.VMEM((PD, C2), BF), pltpu.VMEM((V...]
where the time goes in v7:
time: 56.6 us; the launch traced here: 56.4 us
  Pallas kernels  55.6 us (98%)
  between operations  0.8 us (1%)
    pallas_call x1, Pallas kernels, local(): pl.pallas_call(kernel, out_shape=(pltpu.VMEM((PD, C2), BF), pltpu.VMEM((V...  53.8 us
    pallas_call x1, Pallas kernels, local(): pl.pallas_call(lambda *refs: finish(grad_scale, *refs), out_shape=(jax.Sh...  1.87 us

profile of v7, /device:TPU:1, one launch (start us, length us, event | category | flops | bytes accessed | tf_op | source)
XLA Modules:
  0.0 56.4 jit_solution(6437725905419147054)
XLA Ops:
  0.6 53.8 %shard_map.111 = (bf16[256,256]{1,0:T(8,128)(2,1)S(1)}, f32[1024,128]{1,0:T(8,128)S(1)}, bf16[3,2048,128]{2,1,0:T(8,128)(2,1)S(1)}) custom-call(bf16[1024,128]{1,0:T(8,128)(2,1)} %features_in.1, bf16[27,128,128]{2,1,0:T(8,128)(2,1)} %conv_weight_in.1, bf16[8,128,256]{2,1,0:T(8,128)(2,1)} %down_weight_in.1, s32[27,1024]{1,0:T(8,128)} %neighbour_map_in.1, ...), custom_call_target="tpu_custom_call" | custom-call | tf_op jit(solution)/shard_map/pallas_call | solution.py:449
  54.4 1.9 %shard_map.112 = (bf16[256,256]{1,0:T(8,128)(2,1)}, f32[1024,128]{1,0:T(8,128)}, f32[27,128,128]{2,1,0:T(8,128)}, f32[8,128,256]{2,1,0:T(8,128)}) custom-call(bf16[256,256]{1,0:T(8,128)(2,1)S(1)} %get-tuple-element.7.refs_0_, f32[1024,128]{1,0:T(8,128)S(1)} %get-tuple-element.8.refs_1_, bf16[3,2048,128]{2,1,0:T(8,128)(2,1)S(1)} %get-tuple-element.9.refs_2_), custom_call_target="tpu_custom_call" | custom-call | tf_op jit(solution)/shard_map/pallas_call | solution.py:495

commit v8 on v7

--- a/solution.py
+++ b/solution.py
@@ -104,7 +104,7 @@
     codes_x, wide_x, wide_h, picked, table, pre, hidden, hidden_grad, pre_grad, z_all, back_x, spread_h,
     out_x, in_x, out_h, in_h, out_spread, in_spread, out_gx, in_gx, send_sem, recv_sem,
     terms, got_core, core_sum, got_plane, plane_sum,
-    sum_send, sum_recv,
+    sum_send, sum_recv, child_pick, turned_features,
 ):
     n = lax.axis_size("shard")
     me = lax.axis_index("shard")
@@ -266,6 +266,8 @@
 
     lax.fori_loop(0, EARLY, pick_local, 0)
     pre[...] = dot(features[...], conv_weight[G])
+    child_pick[...] = list_matrix(child_rows[...], CAP2)
+    turned_features[...] = features[...].T
     send_x.wait_recv()
     for s in range(S):
         table[pl.ds(HALF + (s % 2) * CAP, CAP), pl.ds((s // 2) * C, C)] = in_x[s]
@@ -304,8 +306,7 @@
     act = pre[...]
     gate = jax.nn.sigmoid(act)
     hidden[...] = (features[...].astype(F32) + act * gate).astype(BF)
-    child_pick = list_matrix(child_rows[...], CAP2)
-    chosen = t_dot(child_pick, hidden[...]).astype(BF)
+    chosen = t_dot(child_pick[...], hidden[...]).astype(BF)
     for s in range(S):
         out_h[s] = chosen[s * CAP2 : (s + 1) * CAP2]
     send_h = copies(2, out_h, in_h, 1)
@@ -324,12 +325,12 @@
     for o in range(O):
         back_spread = jnp.concatenate([in_spread[s, :, o * C2 : (o + 1) * C2] for s in range(S)], axis=0)
         returned += dot_t(back_spread, down_weight[o])
-    grad_h = hidden_grad[...] + dot(child_pick, returned.astype(BF))
+    grad_h = hidden_grad[...] + dot(child_pick[...], returned.astype(BF))
     hidden_grad[...] = grad_h
     pre_grad[...] = (grad_h * (gate * (1.0 + act * (1.0 - gate)))).astype(BF)
 
     turned_grad = pre_grad[...].T
-    put_block(SELF, t_dot(features[...], pre_grad[...]).astype(BF))
+    put_block(SELF, dot(turned_features[...], pre_grad[...]).astype(BF))
     for k in range(0, G, 2):
         products = dot(turned_grad, jnp.concatenate([picked[k], picked[k + 1]], axis=1))
         for i in range(2):
@@ -401,12 +402,12 @@
     backward_local_group(G - 2, 2)
     hidden_grad[...] += dot_t(pre_grad[...], conv_weight[G])
 
+    sum_turn(4, (2, 0, 1))
     send_gx.wait_recv()
     returned = dot(list_matrix(halo_rows[...], CAP), jnp.concatenate([in_gx[s] for s in range(S)], axis=0))
     local_back = jnp.concatenate([back_x[0:HALF, 0:C], back_x[0:HALF, C : 2 * C]], axis=0)
     input_grad[...] = hidden_grad[...] + local_back + returned
 
-    sum_turn(4, (2, 0, 1))
     sum_turn(5, (2, 0, 1))
     for group in flying:
         group.wait_send()
@@ -486,6 +487,8 @@
             pltpu.VMEM((3, 4, 64, C), F32),
             pltpu.SemaphoreType.DMA((5, 3)),
             pltpu.SemaphoreType.DMA((5, 3)),
+            pltpu.VMEM((V, S * CAP2), BF),
+            pltpu.VMEM((C, V), BF),
         ],
         compiler_params=pltpu.CompilerParams(
             collective_id=0, has_side_effects=True, vmem_limit_bytes=52 * 2**20

time: 56.6 us -> 56.5 us (level)
  no operation moved by 1% of the time
where the time goes in v8:
time: 56.5 us; the launch traced here: 56.3 us
  Pallas kernels  55.5 us (98%)
  between operations  0.8 us (1%)
    pallas_call x1, Pallas kernels, local(): pl.pallas_call(kernel, out_shape=(pltpu.VMEM((PD, C2), BF), pltpu.VMEM((V...  53.7 us
    pallas_call x1, Pallas kernels, local(): pl.pallas_call(lambda *refs: finish(grad_scale, *refs), out_shape=(jax.Sh...  1.87 us

profile of v8, /device:TPU:1, one launch (start us, length us, event | category | flops | bytes accessed | tf_op | source)
XLA Modules:
  0.0 56.3 jit_solution(11913032507815832386)
XLA Ops:
  0.6 53.7 %shard_map.111 = (bf16[256,256]{1,0:T(8,128)(2,1)S(1)}, f32[1024,128]{1,0:T(8,128)S(1)}, bf16[3,2048,128]{2,1,0:T(8,128)(2,1)S(1)}) custom-call(bf16[1024,128]{1,0:T(8,128)(2,1)} %features_in.1, bf16[27,128,128]{2,1,0:T(8,128)(2,1)} %conv_weight_in.1, bf16[8,128,256]{2,1,0:T(8,128)(2,1)} %down_weight_in.1, s32[27,1024]{1,0:T(8,128)} %neighbour_map_in.1, ...), custom_call_target="tpu_custom_call" | custom-call | tf_op jit(solution)/shard_map/pallas_call | solution.py:450
  54.3 1.9 %shard_map.112 = (bf16[256,256]{1,0:T(8,128)(2,1)}, f32[1024,128]{1,0:T(8,128)}, f32[27,128,128]{2,1,0:T(8,128)}, f32[8,128,256]{2,1,0:T(8,128)}) custom-call(bf16[256,256]{1,0:T(8,128)(2,1)S(1)} %get-tuple-element.7.refs_0_, f32[1024,128]{1,0:T(8,128)S(1)} %get-tuple-element.8.refs_1_, bf16[3,2048,128]{2,1,0:T(8,128)(2,1)S(1)} %get-tuple-element.9.refs_2_), custom_call_target="tpu_custom_call" | custom-call | tf_op jit(solution)/shard_map/pallas_call | solution.py:498
